TPU v7x, 256 devices: a whole 4x4x8 slice. The times are simulated.
256 devices in a mesh: dp: 16 (over y_hi, z), head: 16 (over x, y_lo, core).
Axes of the slice: x: 4, y: 4 (y_hi: 2, y_lo: 2; y = y_hi * 2 + y_lo), z: 8, core: 2. Of those that a mesh axis runs over, the one named last changes fastest.
Arguments:
- tokens: bfloat16 [10240, 7168], P('dp', 'head'), may hold values from -40 to 40
- query_latent: bfloat16 [10240, 1536], P('dp'), may hold values from -20 to 20
- keyval_latent: bfloat16 [10240, 512], P('dp'), may hold values from -20 to 20
- query_gain: float32 [1536], replicated, may hold values from 0.5 to 12
- keyval_gain: float32 [512], replicated, may hold values from 0.5 to 12
- query_cotangent: bfloat16 [10240, 24576], P('dp', 'head'), may hold values from -20 to 20
- keyval_cotangent: bfloat16 [10240, 32768], P('dp', 'head'), may hold values from -20 to 20
- master_query_up: float32 [1536, 24576], P('dp', 'head'), may hold values from -0.15625 to 0.15625
- master_keyval_up: float32 [512, 32768], P('dp', 'head'), may hold values from -0.25 to 0.25
- master_query_down: float32 [1536, 7168], P('dp', 'head'), may hold values from -0.0625 to 0.0625
- master_keyval_down: float32 [512, 7168], P('dp', 'head'), may hold values from -0.0625 to 0.0625
- mean_query_up: float32 [1536, 24576], P('dp', 'head'), may hold values from -0.15625 to 0.15625
- mean_keyval_up: float32 [512, 32768], P('dp', 'head'), may hold values from -0.15625 to 0.15625
- mean_query_down: float32 [1536, 7168], P('dp', 'head'), may hold values from -0.75 to 0.75
- mean_keyval_down: float32 [512, 7168], P('dp', 'head'), may hold values from -0.75 to 0.75
- square_query_up: float32 [128], P('head'), may hold values from 0.0001 to 0.001
- square_keyval_up: float32 [128], P('head'), may hold values from 0.0001 to 0.001
- square_query_down: float32 [1536], P('dp'), may hold values from 0.003 to 0.1
- square_keyval_down: float32 [512], P('dp'), may hold values from 0.003 to 0.1
Outputs:
- token_grad: bfloat16 [10240, 7168], P('dp', 'head')
- update_query_up: float32 [1536, 24576], P('dp', 'head')
- update_keyval_up: float32 [512, 32768], P('dp', 'head')
- update_query_down: float32 [1536, 7168], P('dp', 'head')
- update_keyval_down: float32 [512, 7168], P('dp', 'head')
- mean_query_up_next: float32 [1536, 24576], P('dp', 'head')
- mean_keyval_up_next: float32 [512, 32768], P('dp', 'head')
- mean_query_down_next: float32 [1536, 7168], P('dp', 'head')
- mean_keyval_down_next: float32 [512, 7168], P('dp', 'head')
- square_query_up_next: float32 [128], P('head')
- square_keyval_up_next: float32 [128], P('head')
- square_query_down_next: float32 [1536], P('dp')
- square_keyval_down_next: float32 [512], P('dp')
All inputs are finite; a program needn't handle non-finite values.
Results may differ from a plain program's by a relative error of at most 0.024.
Values may be sent and summed in bfloat16 or wider, within the bound.
A program may use at most 128 MiB of HBM per device.

v0:
```python
import jax
import jax.numpy as jnp
from jax import lax
from jax.sharding import PartitionSpec as P

D = 7168
QL = 1536
KVL = 512
QK = 192
KVH = 256


norm_eps = 1e-06
adam_eps = 1e-08
beta_first = 0.9
beta_second = 0.95
adam_step = 10


def normalize(latent, gain):
    values = latent.astype(jnp.float32)
    inverse = lax.rsqrt(jnp.mean(values * values, axis=1, keepdims=True) + norm_eps)
    normed = (values * inverse * gain).astype(jnp.bfloat16)
    return (values, inverse, normed)


def norm_back(values, inverse, gain, upstream):
    weighted = gain * upstream
    inner = jnp.sum(values * weighted, axis=1, keepdims=True) / values.shape[1]
    return (inverse * weighted - values * inverse**3 * inner).astype(jnp.bfloat16)


def rows_product(left, right):
    return lax.dot_general(
        left, right, (((0,), (0,)), ((), ())), preferred_element_type=jnp.float32
    )


def cols_product(left, right):
    return lax.dot_general(
        left, right, (((1,), (1,)), ((), ())), preferred_element_type=jnp.float32
    )


def direction(first_next, second_wide):
    first_scale = 1.0 - beta_first**adam_step
    second_scale = 1.0 - beta_second**adam_step
    return first_next / first_scale / (jnp.sqrt(second_wide / second_scale) + adam_eps)


def moment_first(first, grad):
    return beta_first * first + (1.0 - beta_first) * grad


def moment_second(second, block_mean):
    return beta_second * second + (1.0 - beta_second) * block_mean


def local(
    tokens,
    query_latent,
    keyval_latent,
    query_gain,
    keyval_gain,
    query_cotangent,
    keyval_cotangent,
    master_query_up,
    master_keyval_up,
    master_query_down,
    master_keyval_down,
    mean_query_up,
    mean_keyval_up,
    mean_query_down,
    mean_keyval_down,
    square_query_up,
    square_keyval_up,
    square_query_down,
    square_keyval_down,
):
    whole_query_up, whole_keyval_up, whole_query_down, whole_keyval_down = (
        lax.all_gather(master_query_up.astype(jnp.bfloat16), "dp", axis=0, tiled=True),
        lax.all_gather(master_keyval_up.astype(jnp.bfloat16), "dp", axis=0, tiled=True),
        lax.all_gather(master_query_down.astype(jnp.bfloat16), "dp", axis=0, tiled=True),
        lax.all_gather(master_keyval_down.astype(jnp.bfloat16), "dp", axis=0, tiled=True),
    )
    query_values, query_inverse, query_normed = normalize(query_latent, query_gain)
    keyval_values, keyval_inverse, keyval_normed = normalize(keyval_latent, keyval_gain)
    part_query_up = rows_product(query_normed, query_cotangent)
    part_keyval_up = rows_product(keyval_normed, keyval_cotangent)
    query_upstream = cols_product(query_cotangent, whole_query_up)
    keyval_upstream = cols_product(keyval_cotangent, whole_keyval_up)
    query_total, keyval_total = (
        lax.psum(query_upstream.astype(jnp.bfloat16), "head").astype(jnp.float32),
        lax.psum(keyval_upstream.astype(jnp.bfloat16), "head").astype(jnp.float32),
    )
    query_slope = norm_back(query_values, query_inverse, query_gain, query_total)
    keyval_slope = norm_back(keyval_values, keyval_inverse, keyval_gain, keyval_total)
    token_grad = (
        jnp.dot(query_slope, whole_query_down, preferred_element_type=jnp.float32)
        + jnp.dot(keyval_slope, whole_keyval_down, preferred_element_type=jnp.float32)
    ).astype(jnp.bfloat16)
    part_query_down = rows_product(query_slope, tokens)
    part_keyval_down = rows_product(keyval_slope, tokens)
    grad_query_up, grad_keyval_up, grad_query_down, grad_keyval_down = (
        lax.psum_scatter(
            part_query_up.astype(jnp.bfloat16), "dp", scatter_dimension=0, tiled=True
        ).astype(jnp.float32),
        lax.psum_scatter(
            part_keyval_up.astype(jnp.bfloat16), "dp", scatter_dimension=0, tiled=True
        ).astype(jnp.float32),
        lax.psum_scatter(
            part_query_down.astype(jnp.bfloat16), "dp", scatter_dimension=0, tiled=True
        ).astype(jnp.float32),
        lax.psum_scatter(
            part_keyval_down.astype(jnp.bfloat16), "dp", scatter_dimension=0, tiled=True
        ).astype(jnp.float32),
    )
    token_count = tokens.shape[0] * lax.axis_size("dp")
    grad_query_up = grad_query_up / token_count
    grad_keyval_up = grad_keyval_up / token_count
    grad_query_down = grad_query_down / token_count
    grad_keyval_down = grad_keyval_down / token_count
    query_rows = grad_query_up.shape[0]
    keyval_rows = grad_keyval_up.shape[0]
    local_heads = grad_query_up.shape[1] // QK
    head_query = jnp.sum(
        (grad_query_up * grad_query_up).reshape(query_rows, local_heads, QK), axis=(0, 2)
    )
    head_keyval = jnp.sum(
        (grad_keyval_up * grad_keyval_up).reshape(keyval_rows, local_heads, KVH), axis=(0, 2)
    )
    row_query = jnp.sum(grad_query_down * grad_query_down, axis=1)
    row_keyval = jnp.sum(grad_keyval_down * grad_keyval_down, axis=1)
    head_query, head_keyval = lax.psum((head_query, head_keyval), "dp")
    row_query, row_keyval = lax.psum((row_query, row_keyval), "head")
    square_query_up_next = moment_second(square_query_up, head_query / (QL * QK))
    square_keyval_up_next = moment_second(square_keyval_up, head_keyval / (KVL * KVH))
    square_query_down_next = moment_second(square_query_down, row_query / D)
    square_keyval_down_next = moment_second(square_keyval_down, row_keyval / D)
    mean_query_up_next = moment_first(mean_query_up, grad_query_up)
    mean_keyval_up_next = moment_first(mean_keyval_up, grad_keyval_up)
    mean_query_down_next = moment_first(mean_query_down, grad_query_down)
    mean_keyval_down_next = moment_first(mean_keyval_down, grad_keyval_down)
    update_query_up = direction(mean_query_up_next, jnp.repeat(square_query_up_next, QK)[None, :])
    update_keyval_up = direction(
        mean_keyval_up_next, jnp.repeat(square_keyval_up_next, KVH)[None, :]
    )
    update_query_down = direction(mean_query_down_next, square_query_down_next[:, None])
    update_keyval_down = direction(mean_keyval_down_next, square_keyval_down_next[:, None])
    return (
        token_grad,
        update_query_up,
        update_keyval_up,
        update_query_down,
        update_keyval_down,
        mean_query_up_next,
        mean_keyval_up_next,
        mean_query_down_next,
        mean_keyval_down_next,
        square_query_up_next,
        square_keyval_up_next,
        square_query_down_next,
        square_keyval_down_next,
    )


def solution(mesh):
    return jax.shard_map(
        local,
        mesh=mesh,
        in_specs=(
            P("dp", "head"),
            P("dp", None),
            P("dp", None),
            P(),
            P(),
            P("dp", "head"),
            P("dp", "head"),
            P("dp", "head"),
            P("dp", "head"),
            P("dp", "head"),
            P("dp", "head"),
            P("dp", "head"),
            P("dp", "head"),
            P("dp", "head"),
            P("dp", "head"),
            P("head"),
            P("head"),
            P("dp"),
            P("dp"),
        ),
        out_specs=(
            P("dp", "head"),
            P("dp", "head"),
            P("dp", "head"),
            P("dp", "head"),
            P("dp", "head"),
            P("dp", "head"),
            P("dp", "head"),
            P("dp", "head"),
            P("dp", "head"),
            P("head"),
            P("head"),
            P("dp"),
            P("dp"),
        ),
        check_vma=False,
    )
```

profile of v0, /device:TPU:1, one launch (start us, length us, event | category | flops | bytes accessed | tf_op | source)
XLA Modules:
  0.0 1295.1 jit_solution(1148575412892747128)
XLA Ops:
  7.2 0.0 copy-start
  7.2 0.0 all-gather.8.cloned.1.call-start
  7.2 1.8 convert_element_type.76
  9.0 0.0 all-gather.8.cloned.1.call-update
  9.0 0.0 all-gather.4.cloned.1.call-start
  9.1 1.8 convert_element_type.70
  10.9 0.0 all-gather.4.cloned.1.call-update
  10.9 0.0 all-reduce.5.cloned.1.call-start
  11.0 86.0 %all-gather.8.cloned.1.call-done = bf16[512,2048]{1,0:T(8,128)(2,1)} async-done(((bf16[32,2048]{1,0:T(8,128)(2,1)}), bf16[512,2048]{1,0:T(8,128)(2,1)}) %all-gather.8.cloned.1.call-update) | async-done | bytes 2097168 | tf_op jit(solution)/shard_map/all_gather | solution.py:82
  96.9 4.0 convolution_convert_fusion.4
  101.0 100.1 %all-gather.4.cloned.1.call-done = bf16[1536,1536]{1,0:T(8,128)(2,1)} async-done(((bf16[96,1536]{1,0:T(8,128)(2,1)}), bf16[1536,1536]{1,0:T(8,128)(2,1)}) %all-gather.4.cloned.1.call-update) | async-done | bytes 4718608 | tf_op jit(solution)/shard_map/all_gather | solution.py:81
  201.1 7.5 convolution_convert_fusion.1
  208.6 0.0 all-reduce.5.cloned.1.call-update
  208.6 0.0 all-gather.6.cloned.1.call-start
  208.7 0.8 copy-done.9
  209.5 0.7 convert_element_type.74
  210.2 0.0 all-gather.6.cloned.1.call-update
  210.2 0.0 reduce-scatter.11.cloned.1.call-start
  210.2 128.3 %all-reduce.5.cloned.1.call-done = (bf16[640,1536]{1,0:T(8,128)(2,1)}, bf16[640,512]{1,0:T(8,128)(2,1)}) async-done(((bf16[640,1536]{1,0:T(8,128)(2,1)}, bf16[640,512]{1,0:T(8,128)(2,1)}), (bf16[640,1536]{1,0:T(8,128)(2,1)}, bf16[640,512]{1,0:T(8,128)(2,1)})) %all-reduce.5.cloned.1.call-update) | async-done | bytes 2621456 | tf_op jit(solution)/shard_map/psum | solution.py:93
  338.6 1.5 fusion.11
  340.0 0.0 copy-start.15
  340.0 3.2 fusion
  343.3 1.8 convolution_convert_fusion.5
  345.1 0.0 reduce-scatter.11.cloned.1.call-update
  345.1 0.0 reduce-scatter.9.cloned.1.call-start
  345.2 0.0 copy-start.16
  345.2 3.2 fusion.3
  348.4 1.4 copy-done.1
  349.8 2.6 convolution_convert_fusion.2
  352.4 0.0 reduce-scatter.9.cloned.1.call-update
  352.4 0.0 reduce-scatter.7.cloned.1.call-start
  352.4 3.3 convolution_convert_fusion.3
  355.8 0.0 reduce-scatter.7.cloned.1.call-update
  355.8 0.2 reduce-scatter.5.cloned.1.call-start
  356.0 8.3 convolution_convert_fusion
  364.3 0.0 reduce-scatter.5.cloned.1.call-update
  364.3 0.8 copy-done.12
  365.1 39.9 %all_gather.15 = bf16[512,448]{1,0:T(8,128)(2,1)} all-gather(bf16[32,448]{1,0:T(8,128)(2,1)S(1)} %convert_element_type.80), channel_id=1, replica_groups=mesh['dp'=16,'head'=16] {'dp'}, dimensions={0}, use_global_device_ids=true | all-gather | bytes 487424 | tf_op jit(solution)/shard_map/all_gather | solution.py:84
  405.1 17.1 %all-gather.6.cloned.1.call-done = bf16[1536,448]{1,0:T(8,128)(2,1)} async-done(((bf16[96,448]{1,0:T(8,128)(2,1)}), bf16[1536,448]{1,0:T(8,128)(2,1)}) %all-gather.6.cloned.1.call-update) | async-done | bytes 1376272 | tf_op jit(solution)/shard_map/all_gather | solution.py:83
  422.2 3.4 fusion.39
  425.6 1.7 fusion.10
  427.3 191.1 %reduce-scatter.11.cloned.1.call-done = bf16[32,448]{1,0:T(8,128)(2,1)} async-done(((bf16[512,448]{1,0:T(8,128)(2,1)}), bf16[32,448]{1,0:T(8,128)(2,1)}) %reduce-scatter.11.cloned.1.call-update) | async-done | bytes 28688 | tf_op jit(solution)/shard_map/reduce_scatter | solution.py:114
  618.4 0.9 fusion.32
  619.3 206.9 %reduce-scatter.9.cloned.1.call-done = bf16[96,448]{1,0:T(8,128)(2,1)} async-done(((bf16[1536,448]{1,0:T(8,128)(2,1)}), bf16[96,448]{1,0:T(8,128)(2,1)}) %reduce-scatter.9.cloned.1.call-update) | async-done | bytes 86032 | tf_op jit(solution)/shard_map/reduce_scatter | solution.py:111
  826.2 1.0 fusion.29
  827.2 32.4 %all-reduce = (f32[96]{0:T(128)S(1)}, f32[32]{0:T(128)S(1)}) all-reduce(f32[96]{0:T(128)S(1)} %fusion.29, f32[32]{0:T(128)S(1)} %fusion.32), channel_id=1, replica_groups=mesh['dp'=16,'head'=16] {'head'}, use_global_device_ids=true, to_apply=%region_16.0 | all-reduce | flops 128 | bytes 1024 | tf_op jit(solution)/shard_map/psum | solution.py:135
  859.6 1.2 sqrt_add_fusion.1
  860.7 1.2 sqrt_add_fusion
  861.9 1.7 multiply_divide_fusion.2
  863.6 168.6 %reduce-scatter.7.cloned.1.call-done = bf16[32,2048]{1,0:T(8,128)(2,1)} async-done(((bf16[512,2048]{1,0:T(8,128)(2,1)}), bf16[32,2048]{1,0:T(8,128)(2,1)}) %reduce-scatter.7.cloned.1.call-update) | async-done | bytes 131088 | tf_op jit(solution)/shard_map/reduce_scatter | solution.py:108
  1032.1 1.0 fusion.26
  1033.2 0.1 reduce_sum.95
  1033.3 216.7 %reduce-scatter.5.cloned.1.call-done = bf16[96,1536]{1,0:T(8,128)(2,1)} async-done(((bf16[1536,1536]{1,0:T(8,128)(2,1)}), bf16[96,1536]{1,0:T(8,128)(2,1)}) %reduce-scatter.5.cloned.1.call-update) | async-done | bytes 294928 | tf_op jit(solution)/shard_map/reduce_scatter | solution.py:105
  1250.0 1.1 fusion.23
  1251.0 0.1 reduce_sum.91
  1251.1 0.1 reduce_sum.92
  1251.2 1.5 multiply_divide_fusion.3
  1252.7 31.1 %all-reduce.1 = (f32[8]{0:T(128)S(1)}, f32[8]{0:T(128)S(1)}) all-reduce(f32[8]{0:T(128)S(1)} %reduce_sum.92, f32[8]{0:T(128)S(1)} %reduce_sum.95), channel_id=1, replica_groups=mesh['dp'=16,'head'=16] {'dp'}, use_global_device_ids=true, to_apply=%region_9.0 | all-reduce | flops 16 | bytes 128 | tf_op jit(solution)/shard_map/psum | solution.py:134
  1283.8 1.2 sqrt_add_fusion.2
  1285.0 0.1 broadcast_in_dim.4
  1285.1 0.1 add.118
  1285.2 0.1 broadcast_bitcast_fusion
  1285.2 2.1 multiply_divide_fusion
  1287.4 0.8 multiply_divide_fusion.1
  (35 shorter events, 0.1 us)
Async XLA Ops:
  7.2 89.8 %copy-start = (bf16[640,2048]{1,0:T(8,128)(2,1)S(1)}, bf16[640,2048]{1,0:T(8,128)(2,1)}, u32[]{:S(2)}) copy-start(bf16[640,2048]{1,0:T(8,128)(2,1)} %param.25) | copy-start | bytes 7864324
  7.2 89.7 %all-gather.8.cloned.1.call-start = ((), (), s32[]{:S(2)}) async-start(), calls=%async_computation.6 | async-start | bytes 2228224 | tf_op jit(solution)/shard_map/all_gather | solution.py:82
  9.0 192.1 %all-gather.4.cloned.1.call-start = ((), (), s32[]{:S(2)}) async-start(), calls=%async_computation.4 | async-start | bytes 5013504 | tf_op jit(solution)/shard_map/all_gather | solution.py:81
  10.9 327.6 %all-reduce.5.cloned.1.call-start = ((), (), s32[]{:S(2)}) async-start(), calls=%async_computation.11 | async-start | bytes 5242880 | tf_op jit(solution)/shard_map/psum | solution.py:93
  208.6 0.9 copy-start.9
  208.6 130.0 %copy-start.2 = (bf16[640,512]{1,0:T(8,128)(2,1)S(1)}, bf16[640,512]{1,0:T(8,128)(2,1)}, u32[]{:S(2)}) copy-start(bf16[640,512]{1,0:T(8,128)(2,1)} %param.21) | copy-start | bytes 1966084
  208.6 130.0 %copy-start.14 = (f32[512]{0:T(512)S(1)}, f32[512]{0:T(512)}, u32[]{:S(2)}) copy-start(f32[512]{0:T(512)} %param.23) | copy-start | bytes 6148
  208.6 131.4 %copy-start.13 = (f32[1536]{0:T(1024)S(1)}, f32[1536]{0:T(1024)}, u32[]{:S(2)}) copy-start(f32[1536]{0:T(1024)} %param.22) | copy-start | bytes 18436
  208.6 213.5 %all-gather.6.cloned.1.call-start = ((), (), s32[]{:S(2)}) async-start(), calls=%async_computation.5 | async-start | bytes 1671168 | tf_op jit(solution)/shard_map/all_gather | solution.py:83
  210.2 408.2 %reduce-scatter.11.cloned.1.call-start = ((), (), s32[]{:S(2)}) async-start(), calls=%async_computation.10 | async-start | bytes 557056 | tf_op jit(solution)/shard_map/reduce_scatter | solution.py:114
  340.0 3.3 copy-start.3
  340.0 3.3 copy-start.15
  345.1 481.0 %reduce-scatter.9.cloned.1.call-start = ((), (), s32[]{:S(2)}) async-start(), calls=%async_computation.9 | async-start | bytes 1671168 | tf_op jit(solution)/shard_map/reduce_scatter | solution.py:111
  345.2 4.6 copy-start.16
  348.4 1.4 copy-start.1
  352.4 679.7 %reduce-scatter.7.cloned.1.call-start = ((), (), s32[]{:S(2)}) async-start(), calls=%async_computation.8 | async-start | bytes 2228224 | tf_op jit(solution)/shard_map/reduce_scatter | solution.py:108
  355.8 894.2 %reduce-scatter.5.cloned.1.call-start = ((), (), s32[]{:S(2)}) async-start(), calls=%async_computation.7 | async-start | bytes 5013504 | tf_op jit(solution)/shard_map/reduce_scatter | solution.py:105
  364.3 0.8 copy-start.12
  422.2 3.4 copy-start.4
  422.2 3.4 copy-start.7
  425.6 436.3 %copy-start.10 = (f32[96,448]{1,0:T(8,128)S(1)}, f32[96,448]{1,0:T(8,128)}, u32[]{:S(2)}) copy-start(f32[96,448]{1,0:T(8,128)} %param.32) | copy-start | bytes 516100
  425.6 825.6 %copy-start.11 = (f32[32,448]{1,0:T(8,128)S(1)}, f32[32,448]{1,0:T(8,128)}, u32[]{:S(2)}) copy-start(f32[32,448]{1,0:T(8,128)} %param.33) | copy-start | bytes 172036
  427.3 857.9 %copy-start.5 = (f32[96,1536]{1,0:T(8,128)S(1)}, f32[96,1536]{1,0:T(8,128)}, u32[]{:S(2)}) copy-start(f32[96,1536]{1,0:T(8,128)} %param.30) | copy-start | bytes 1769476
  1032.1 255.3 %copy-start.6 = (bf16[32,2048]{1,0:T(8,128)(2,1)S(1)}, bf16[32,2048]{1,0:T(8,128)(2,1)}, u32[]{:S(2)}) copy-start(bf16[32,2048]{1,0:T(8,128)(2,1)} %reduce-scatter.7.cloned.1.call-done) | copy-start | bytes 393220
  1285.2 2.2 copy-start.8
Sparse Core Ops, SparseCore 0:
  11.2 85.7 all-gather.7
  100.1 100.9 all-gather.3
  208.8 129.7 all-reduce.4
  341.6 80.5 all-gather.5
  426.4 191.9 reduce-scatter.10
  622.6 203.4 reduce-scatter.8
  830.1 202.0 reduce-scatter.6
  1036.2 213.7 reduce-scatter.4
where the time goes:
time: 1310 us; the launch traced here: 1300 us
  waiting for transfers between devices  1110 us (85%)
  blocking collectives  103 us (8%)
  matrix products  32.6 us (2%)
  other arithmetic  26 us (2%)
  between operations  14.3 us (1%)
    reduce_scatter x1, waiting for transfers between devices, local(): lax.psum_scatter(part_query_up.astype(jnp.bfloat16), 'dp', scatter_dimens...  217 us
    reduce_scatter x1, waiting for transfers between devices, local(): lax.psum_scatter(part_query_down.astype(jnp.bfloat16), 'dp', scatter_dime...  207 us
    reduce_scatter x1, waiting for transfers between devices, local(): lax.psum_scatter(part_keyval_down.astype(jnp.bfloat16), 'dp', scatter_dim...  191 us
    reduce_scatter x1, waiting for transfers between devices, local(): lax.psum_scatter(part_keyval_up.astype(jnp.bfloat16), 'dp', scatter_dimen...  169 us
    psum x1, waiting for transfers between devices, local(): lax.psum(query_upstream.astype(jnp.bfloat16), 'head').astype(jnp.float32)  128 us
    all_gather x1, waiting for transfers between devices, local(): lax.all_gather(master_query_up.astype(jnp.bfloat16), 'dp', axis=0, tiled=...  100 us
    all_gather x1, waiting for transfers between devices, local(): lax.all_gather(master_keyval_up.astype(jnp.bfloat16), 'dp', axis=0, tiled...  86 us
    all_gather x1, blocking collectives, local(): lax.all_gather(master_keyval_down.astype(jnp.bfloat16), 'dp', axis=0, til...  39.9 us
  transfers between devices with their start and end apart: 8, of which 8 were waited for; matrix products, arithmetic and copies ran while one was open for 3% of the time, Pallas kernels for 0%

commit v1 on v0

v1 whole, which is shorter than its diff:
```python
import jax
import jax.numpy as jnp
from jax import lax
from jax.experimental import pallas as pl
from jax.experimental.pallas import tpu as pltpu
from jax.sharding import PartitionSpec as P

D = 7168
QL = 1536
KVL = 512
QK = 192
KVH = 256
TOKENS = 10240
TOK = 640

NZ = 8
NX = 4
DC = 448
QR, KR, DR = 96, 32, 128
GQ, GK, GW = 4 * QR, 4 * KR, 4 * (QR + KR)
QC, KC = 1536, 2048
SLICE = 80

norm_eps = 1e-06
adam_eps = 1e-08
beta_first = 0.9
beta_second = 0.95
adam_step = 10
first_scale = 1.0 - beta_first**adam_step
second_scale = 1.0 - beta_second**adam_step

MESH = pl.DeviceIdType.MESH
f32 = jnp.float32
bf16 = jnp.bfloat16
N_SEM = 192


def place(rel, d):
    d = d % NZ
    if d == 0 or d == NZ // 2:
        return (0, rel * 2 + (1 if d else 0))
    if d < NZ // 2:
        return (d, rel * 2)
    return (NZ - d, rel * 2 + 1)


def split3(a):
    hi = a.astype(bf16)
    rest = a - hi.astype(f32)
    mid = rest.astype(bf16)
    low = (rest - mid.astype(f32)).astype(bf16)
    return hi, mid, low


def dot(a, b):
    return jnp.dot(a, b, preferred_element_type=f32)


def dot_t(a, b):
    return lax.dot_general(a, b, (((1,), (1,)), ((), ())), preferred_element_type=f32)


def select_dot(a, chosen):
    hi, mid, low = split3(a)
    return dot(hi, chosen) + dot(mid, chosen) + dot(low, chosen)


def loop(count, body):
    def step(i, carry):
        body(i)
        return carry

    lax.fori_loop(0, count, step, 0)


def total(refs, rows):
    parts = [r[rows, :].astype(f32) for r in refs]
    out = parts[0]
    for p in parts[1:]:
        out = out + p
    return out


def add_into(refs, out, start, rows):
    def body(i):
        at = pl.ds(pl.multiple_of(start + i * 16, 16), 16)
        out[at, :] = total(refs, at).astype(out.dtype)

    loop(rows // 16, body)


def kernel(
    tok_h, lq_h, lk_h, gq_ref, gk_ref, cq_h, ck_h,
    mq_h, mk_h, mdq_h, mdk_h, eq_h, ek_h, edq_h, edk_h,
    sq_ref, sk_ref, sdq_ref, sdk_ref,
    tg_h, uq_h, uk_h, udq_h, udk_h, nq_h, nk_h, ndq_h, ndk_h,
    osq_ref, osk_ref, osdq_ref, osdk_ref,
    tok, lq, lk, cq, ck, mq, mk, md, eq, ek, ed,
    wq, wk, wd, pq, pk, pd, yq, yk, yd, zq, zk, zd,
    normq, normk, turned, up, core_in, half, x_in, mine, pair_in, full,
    latent, gains, slope, tg, small, small_pair, small_z, small_row, small_core, small_lo, small_x,
    send_sems, recv_sems, local_sems,
):
    dp = lax.axis_index("dp")
    hd = lax.axis_index("head")
    yh, z = dp // NZ, dp % NZ
    x, yl, c = hd // 4, (hd // 2) % 2, hd % 2

    def z_dev(k):
        return (yh * NZ + (z + k + NZ) % NZ, hd)

    def x_dev(k):
        return (dp, ((x + k + NX) % NX) * 4 + yl * 2 + c)

    other_half = ((1 - yh) * NZ + z, hd)
    other_low = (dp, x * 4 + (1 - yl) * 2 + c)
    other_core = (dp, x * 4 + yl * 2 + 1 - c)
    z_next = (z_dev(1), z_dev(-1))
    x_next = (x_dev(1), x_dev(-1))

    ids = {}
    sent = []

    def remote(key, src, dst, dev):
        i = ids.setdefault(key, len(ids))
        return pltpu.make_async_remote_copy(
            src_ref=src, dst_ref=dst, send_sem=send_sems.at[i], recv_sem=recv_sems.at[i],
            device_id=dev, device_id_type=MESH,
        )

    def send(key, src, dst, dev):
        copy = remote(key, src, dst, dev)
        copy.start()
        sent.append(copy)

    def recv(key, land):
        remote(key, land, land, other_core).wait_recv()

    n_local = [0]

    def fetch(src, dst):
        copy = pltpu.make_async_copy(src, dst, local_sems.at[n_local[0]])
        n_local[0] += 1
        copy.start()
        return copy

    l_mk, l_mq = fetch(mk_h, mk), fetch(mq_h, mq)
    l_lk, l_ck = fetch(lk_h, lk), fetch(ck_h, ck)
    l_lq, l_cq = fetch(lq_h, lq), fetch(cq_h, cq)
    l_md = (fetch(mdq_h, md.at[pl.ds(0, QR)]), fetch(mdk_h, md.at[pl.ds(QR, KR)]))
    l_tok = fetch(tok_h, tok)
    l_eq, l_ek = fetch(eq_h, eq), fetch(ek_h, ek)
    l_ed = (fetch(edq_h, ed.at[pl.ds(0, QR)]), fetch(edk_h, ed.at[pl.ds(QR, KR)]))

    barrier = pltpu.get_barrier_semaphore()
    peers = [z_dev(k) for k in range(1, NZ)] + [x_dev(k) for k in range(1, NX)]
    peers += [other_half, other_low, other_core]
    for dev in peers:
        pl.semaphore_signal(barrier, inc=1, device_id=dev, device_id_type=MESH)

    def round_rows(src, dst, rows):
        def body(i):
            at = pl.ds(pl.multiple_of(i * 16, 16), 16)
            dst[at, :] = src[at, :].astype(bf16)

        loop(rows // 16, body)

    gathered = {"k": (wk, KR), "q": (wq, QR), "d": (wd, DR)}

    def gather_pair(w):
        ref, _ = gathered[w]
        send(("y", w), ref.at[place(0, 0)], ref.at[place(1, 0)], other_half)

    def gather_first(w, rel):
        ref, _ = gathered[w]
        if rel:
            recv(("y", w), ref.at[place(1, 0)])
        for side, sign in ((0, -1), (1, 1)):
            send(("g", w, rel, 1, side), ref.at[place(rel, 0)], ref.at[place(rel, sign)], z_next[side])

    def gather_next(w, rel, step):
        ref, rows = gathered[w]
        h = rows // 2
        for side, sign in ((0, -1), (1, 1)):
            here = ref.at[place(rel, sign * step)]
            if step == 4:
                recv(("g", w, rel, 4, side), here.at[pl.ds(side * h, h)])
                continue
            recv(("g", w, rel, step, side), here)
            there = ref.at[place(rel, sign * (step + 1))]
            if step == 3:
                here, there = here.at[pl.ds(side * h, h)], there.at[pl.ds(side * h, h)]
            send(("g", w, rel, step + 1, side), here, there, z_next[side])

    def own_block(ref, half_of, d):
        return ref.at[half_of * NZ + (z + d) % NZ]

    scattered = {
        "k": (lambda d: own_block(pk, yh, d), lambda d: own_block(pk, 1 - yh, d), yk, zk, KR),
        "q": (lambda d: own_block(pq, yh, d), lambda d: own_block(pq, 1 - yh, d), yq, zq, QR),
        "d": (lambda d: pd.at[place(0, d)], lambda d: pd.at[place(1, d)], yd, zd, DR),
    }

    def scatter_pair(w, d):
        _, theirs, y, _, _ = scattered[w]
        send(("sy", w, d), theirs(d), y.at[d], other_half)

    def scatter_first(w):
        own, _, y, zz, rows = scattered[w]
        h = rows // 2
        recv(("sy", w, 4), y.at[4])
        add_into([own(4), y.at[4]], own(4), 0, rows)
        for side in range(2):
            at = pl.ds(side * h, h)
            send(("s", w, 0, side), own(4).at[at], zz.at[side, 0].at[at], z_next[side])

    def scatter_next(w, step):
        own, _, y, zz, rows = scattered[w]
        h = rows // 2
        for side in range(2):
            d = 3 - step if side == 0 else 5 + step
            recv(("sy", w, d), y.at[d])
            if step == 0:
                came = zz.at[side, 0]
                recv(("s", w, 0, side), came.at[pl.ds(side * h, h)])
                add_into([own(d), y.at[d], came], own(d), side * h, h)
                add_into([own(d), y.at[d]], own(d), (1 - side) * h, h)
            else:
                came = zz.at[side, step]
                recv(("s", w, step, side), came)
                add_into([own(d), y.at[d], came], own(d), 0, rows)
            send(("s", w, step + 1, side), own(d), zz.at[side, step + 1], z_next[side])

    def scatter_last(w):
        own, _, y, zz, _ = scattered[w]
        recv(("sy", w, 0), y.at[0])
        recv(("s", w, 3, 0), zz.at[0, 3])
        recv(("s", w, 3, 1), zz.at[1, 3])
        return [own(0), y.at[0], zz.at[0, 3], zz.at[1, 3]]

    l_mk.wait()
    round_rows(mk, wk.at[place(0, 0)], KR)
    l_mq.wait()
    round_rows(mq, wq.at[place(0, 0)], QR)
    pl.semaphore_wait(barrier, len(peers))
    gather_pair("k")
    gather_first("k", 0)
    gather_pair("q")
    gather_first("q", 0)
    for load in l_md:
        load.wait()
    round_rows(md, wd.at[place(0, 0)], DR)

    def normalize(src, gain_ref, dst, width):
        def body(i):
            at = pl.ds(pl.multiple_of(i * 16, 16), 16)
            values = src[at, :].astype(f32)
            inverse = lax.rsqrt(jnp.sum(values * values, axis=1, keepdims=True) / width + norm_eps)
            dst[at, :] = (values * inverse * gain_ref[...]).astype(bf16)

        loop(TOK // 16, body)

    def turn(src, start, width):
        def body(i):
            at = pl.ds(pl.multiple_of(i * 128, 128), 128)
            block = src[at, pl.ds(start, width)]
            turned[pl.ds(0, width), at] = block.T

        loop(TOK // 128, body)

    def part_keyval(half_of):
        turn(normk, pl.multiple_of(half_of * 256, 128), 256)

        def body(i):
            at = pl.ds(pl.multiple_of(i * 512, 512), 512)
            out = dot(turned[pl.ds(0, 256), :], ck[:, at]).astype(bf16)
            pk[pl.ds(half_of * NZ, NZ), :, at] = out.reshape(NZ, KR, 512)

        loop(KC // 512, body)

    def part_query(half_of):
        def chunk(q):
            turn(normq, pl.multiple_of(half_of * 768 + q * GQ, 128), GQ)

            def body(i):
                at = pl.ds(pl.multiple_of(i * 512, 512), 512)
                out = dot(turned[pl.ds(0, GQ), :], cq[:, at]).astype(bf16)
                pq[pl.ds(half_of * NZ + q * 4, 4), :, at] = out.reshape(4, QR, 512)

            loop(QC // 512, body)

        loop(2, chunk)

    order = (4, 3, 5, 2, 6, 1, 7, 0)
    l_lk.wait()
    normalize(lk, gk_ref, normk, KVL)
    l_ck.wait()
    part_keyval(1 - yh)
    for d in order[:3]:
        scatter_pair("k", d)
    l_lq.wait()
    normalize(lq, gq_ref, normq, QL)
    gather_first("k", 1)
    l_cq.wait()
    part_query(1 - yh)
    gather_first("q", 1)
    for i, d in enumerate(order):
        scatter_pair("q", d)
        if i >= 3:
            scatter_pair("k", d)
    gather_pair("d")
    part_keyval(yh)
    part_query(yh)

    first_token = pl.multiple_of(c * (TOK // 2) + x * SLICE, 16)

    def arrange(src, gain_ref, rows, natural, width, group, at):
        lane = lax.broadcasted_iota(jnp.int32, (1, 4 * rows), 1)
        j = sum((lane >= rows * k).astype(jnp.int32) for k in (1, 2, 3))
        inside = lane - j * rows
        rel, back = j // 2, j % 2
        d = back * (NZ // 2) if group == 0 else jnp.where(back == 1, NZ - group, group)
        owner = jnp.where(rel == 1, 1 - yh, yh) * NZ + (z + d) % NZ
        source = owner * rows + inside
        chosen = (lax.broadcasted_iota(jnp.int32, (width, 4 * rows), 0) == source).astype(f32).astype(bf16)
        latent[group, :, at] = dot(src[pl.ds(first_token, SLICE), :], chosen)
        gain = jnp.broadcast_to(gain_ref[...], (8, width))
        gains[group, :, at] = select_dot(gain, chosen)

    for g in range(4):
        arrange(lq, gq_ref, QR, 0, QL, g, pl.ds(0, GQ))
        arrange(lk, gk_ref, KR, 0, KVL, g, pl.ds(GQ, GK))

    def upstream(g):
        def body(i):
            at = pl.ds(pl.multiple_of(i * 160, 160), 160)
            up[g, at, pl.ds(0, GQ)] = dot_t(cq[at, :], wq[g].reshape(GQ, QC)).astype(bf16)
            up[g, at, pl.ds(GQ, GK)] = dot_t(ck[at, :], wk[g].reshape(GK, KC)).astype(bf16)

        loop(TOK // 160, body)
        there = pl.ds(pl.multiple_of((1 - c) * 320, 16), 320)
        send(("c", g), up.at[g, there], core_in.at[g], other_core)

    def after_core(g):
        recv(("c", g), core_in.at[g])
        here = up.at[g, pl.ds(pl.multiple_of(c * 320, 16), 320)]
        add_into([here, core_in.at[g]], half.at[g], 0, 320)
        for k in (2, 1, 3):
            to = (x + k) % NX
            send(("x", g, k), half.at[g, pl.ds(pl.multiple_of(to * SLICE, 16), SLICE)], x_in.at[g, k - 1], x_dev(k))

    def after_x(g):
        for k in range(1, NX):
            recv(("x", g, k), x_in.at[g, k - 1])
        here = half.at[g, pl.ds(pl.multiple_of(x * SLICE, 16), SLICE)]
        add_into([here] + [x_in.at[g, k] for k in range(NX - 1)], mine.at[g], 0, SLICE)
        send(("l", g), mine.at[g], pair_in.at[g], other_low)

    def after_low(g):
        recv(("l", g), pair_in.at[g])
        add_into([mine.at[g], pair_in.at[g]], full.at[g], 0, SLICE)

    for step in (1, 2, 3):
        for rel in range(2):
            for w in ("k", "q"):
                gather_next(w, rel, step)
        upstream(step)
        if step > 1:
            after_x(step - 1)
        if step > 2:
            after_low(step - 2)
        after_core(step)

    after_x(3)
    after_low(2)
    for w in ("k", "q"):
        gather_next(w, 0, 4)
    scatter_first("k")
    for w in ("k", "q"):
        gather_next(w, 1, 4)
    scatter_first("q")
    upstream(0)
    gather_first("d", 0)
    gather_first("d", 1)
    after_low(3)
    scatter_next("k", 0)
    after_core(0)
    scatter_next("q", 0)
    for rel in range(2):
        gather_next("d", rel, 1)
    after_x(0)
    scatter_next("k", 1)
    after_low(0)

    own_rows = pl.ds(first_token, SLICE)

    def norm_back(i):
        at = pl.ds(pl.multiple_of(i * 16, 16), 16)
        to = pl.ds(pl.multiple_of(first_token + i * 16, 16), 16)
        for first, width, units in ((0, GQ, QL), (GQ, GK, KVL)):
            cols = pl.ds(first, width)
            squares = 0.0
            inner = 0.0
            for g in range(4):
                values = latent[g, at, cols]
                squares += jnp.sum(values * values, axis=1, keepdims=True)
                inner += jnp.sum(values * gains[g, pl.ds(0, 1), cols] * full[g, at, cols], axis=1, keepdims=True)
            inverse = lax.rsqrt(squares / units + norm_eps)
            scale = inverse * inverse * inverse * (inner / units)
            for g in range(4):
                weighted = gains[g, pl.ds(0, 1), cols] * full[g, at, cols]
                slope[to, pl.ds(g * GW + first, width)] = (inverse * weighted - latent[g, at, cols] * scale).astype(bf16)

    loop(SLICE // 16, norm_back)

    sides = (pl.ds(0, 2 * GW), pl.ds(2 * GW, 2 * GW))

    def block_rows(k, core):
        return pl.ds(pl.multiple_of(core * 320 + ((x + k + NX) % NX) * SLICE, 16), SLICE)

    for part in range(2):
        for side in range(2):
            cols = sides[part if side == 0 else 1 - part]
            view = slope.at[own_rows, cols]
            send(("a", 1, side, part), view, view, x_next[side])
    view = slope.at[own_rows, :]
    send(("ac", 0), view, view, other_core)
    scatter_next("q", 1)
    for side, back in ((0, -1), (1, 1)):
        view = slope.at[block_rows(back, c), sides[side]]
        recv(("a", 1, side, 0), view)
        send(("a", 2, side), view, view, x_next[side])
    for rel in range(2):
        gather_next("d", rel, 2)
    scatter_next("k", 2)
    for side, back in ((0, -1), (1, 1)):
        recv(("a", 1, side, 1), slope.at[block_rows(back, c), sides[1 - side]])
        view = slope.at[block_rows(back, c), :]
        send(("ac", 1 + side), view, view, other_core)
    for side in range(2):
        recv(("a", 2, side), slope.at[block_rows(2, c), sides[side]])
    view = slope.at[block_rows(2, c), :]
    send(("ac", 3), view, view, other_core)
    for i, k in enumerate((0, -1, 1, 2)):
        recv(("ac", i), slope.at[block_rows(k, 1 - c), :])

    l_tok.wait()
    for g in range(4):
        turn(slope, g * GW, GW)
        out = dot_t(turned[...], tok[...]).astype(bf16)
        pd[g, :, pl.ds(0, QR), :] = out[:GQ].reshape(4, QR, DC)
        pd[g, :, pl.ds(QR, KR), :] = out[GQ:].reshape(4, KR, DC)
    for d in order:
        scatter_pair("d", d)
    scatter_next("q", 2)
    for rel in range(2):
        gather_next("d", rel, 3)

    def finish(refs, grad, mean, rows, cols):
        def step(i, squares):
            at = pl.ds(pl.multiple_of(i * 16, 16), 16)
            g = total(refs, at) / TOKENS
            mean[at, :] = beta_first * mean[at, :] + (1.0 - beta_first) * g
            return squares + g[0:8] * g[0:8] + g[8:16] * g[8:16]

        return lax.fori_loop(0, rows // 16, step, jnp.zeros((8, cols), f32))

    def heads_of(width, per_head):
        col = lax.broadcasted_iota(jnp.int32, (width, 128), 0)
        head = lax.broadcasted_iota(jnp.int32, (width, 128), 1)
        return ((col >= head * per_head) & (col < (head + 1) * per_head)).astype(f32).astype(bf16)

    def columns_of(width, per_head):
        head = lax.broadcasted_iota(jnp.int32, (128, width), 0)
        col = lax.broadcasted_iota(jnp.int32, (128, width), 1)
        return ((col >= head * per_head) & (col < (head + 1) * per_head)).astype(f32).astype(bf16)

    l_ek.wait()
    squares_k = finish(scatter_last("k"), None, ek, KR, KC)
    heads_k = jnp.sum(select_dot(squares_k, heads_of(KC, KVH)), axis=0, keepdims=True) / (KVL * KVH)
    scatter_first("d")
    l_eq.wait()
    squares_q = finish(scatter_last("q"), None, eq, QR, QC)
    heads_q = jnp.sum(select_dot(squares_q, heads_of(QC, QK)), axis=0, keepdims=True) / (QL * QK)
    row8 = lax.broadcasted_iota(jnp.int32, (8, 128), 0)
    small[...] = jnp.where(row8 == 0, heads_q, jnp.where(row8 == 1, heads_k, 0.0))
    send(("hy",), small, small_pair, other_half)
    scatter_next("d", 0)
    recv(("hy",), small_pair)
    small_z[0] = small[...] + small_pair[...]
    for k in range(1, NZ):
        send(("hz", k), small_z.at[0], small_z.at[k], z_dev(k))

    for rel in range(2):
        gather_next("d", rel, 4)

    def token_grad(i):
        at = pl.ds(pl.multiple_of(i * 128, 128), 128)
        out = jnp.zeros((128, DC), f32)
        for g in range(4):
            out += dot(slope[at, pl.ds(g * GW, GQ)], wd[g, :, pl.ds(0, QR), :].reshape(GQ, DC))
            out += dot(slope[at, pl.ds(g * GW + GQ, GK)], wd[g, :, pl.ds(QR, KR), :].reshape(GK, DC))
        tg[:, at] = out.T.astype(bf16)

    loop(TOK // 128, token_grad)
    stores = [fetch(tg, tg_h)]
    scatter_next("d", 1)

    for k in range(1, NZ):
        recv(("hz", k), small_z.at[k])
    heads = small_z[0]
    for k in range(1, NZ):
        heads = heads + small_z[k]
    small_row[...] = jnp.zeros((8, 128), f32)
    small_row[pl.ds(0, 1), pl.ds(0, 8)] = sq_ref[...]
    small_row[pl.ds(1, 1), pl.ds(0, 8)] = sk_ref[...]
    second = beta_second * small_row[...] + (1.0 - beta_second) * heads
    osq_ref[...] = second[0:1, 0:8]
    osk_ref[...] = second[1:2, 0:8]

    def update(second_wide, mean, out, rows):
        factor = 1.0 / (jnp.sqrt(second_wide / second_scale) + adam_eps)

        def body(i):
            at = pl.ds(pl.multiple_of(i * 16, 16), 16)
            out[at, :] = mean[at, :] / first_scale * factor

        loop(rows // 16, body)

    update(select_dot(second, columns_of(QC, QK))[0:1], eq, mq, QR)
    update(select_dot(second, columns_of(KC, KVH))[1:2], ek, mk, KR)
    stores += [fetch(eq, nq_h), fetch(ek, nk_h), fetch(mq, uq_h), fetch(mk, uk_h)]

    scatter_next("d", 2)
    eye = lax.broadcasted_iota(jnp.int32, (128, 128), 0) == lax.broadcasted_iota(jnp.int32, (128, 128), 1)
    small_row[...] = jnp.zeros((8, 128), f32)
    small_row[pl.ds(0, 1), pl.ds(0, QR)] = sdq_ref[...]
    small_row[pl.ds(0, 1), pl.ds(QR, KR)] = sdk_ref[...]
    old = small_row[pl.ds(0, 1), :]
    for load in l_ed:
        load.wait()
    grad = total(scatter_last("d"), slice(None)) / TOKENS
    mean_next = beta_first * ed[...] + (1.0 - beta_first) * grad
    ed[...] = mean_next
    column = jnp.sum(grad * grad, axis=1, keepdims=True) / D
    row = jnp.sum(jnp.where(eye, column, 0.0), axis=0, keepdims=True)
    small_core[0] = jnp.broadcast_to(row, (8, 128))
    send(("rc",), small_core.at[0], small_core.at[1], other_core)
    stores += [fetch(ed.at[pl.ds(0, QR)], ndq_h), fetch(ed.at[pl.ds(QR, KR)], ndk_h)]
    recv(("rc",), small_core.at[1])
    small_lo[0] = small_core[0] + small_core[1]
    send(("rl",), small_lo.at[0], small_lo.at[1], other_low)
    recv(("rl",), small_lo.at[1])
    small_x[0] = small_lo[0] + small_lo[1]
    for k in range(1, NX):
        send(("rx", k), small_x.at[0], small_x.at[k], x_dev(k))
    for k in range(1, NX):
        recv(("rx", k), small_x.at[k])
    rows_total = (small_x[0] + small_x[1]) + (small_x[2] + small_x[3])
    second_row = beta_second * old + (1.0 - beta_second) * rows_total[0:1]
    osdq_ref[...] = second_row[:, 0:QR]
    osdk_ref[...] = second_row[:, QR:DR]
    second_col = jnp.sum(jnp.where(eye, second_row, 0.0), axis=1, keepdims=True)
    factor = 1.0 / (jnp.sqrt(second_col / second_scale) + adam_eps)
    md[...] = mean_next / first_scale * factor
    stores += [fetch(md.at[pl.ds(0, QR)], udq_h), fetch(md.at[pl.ds(QR, KR)], udk_h)]

    for copy in sent:
        copy.wait_send()
    for store in stores:
        store.wait()


def local(*args):
    (
        tokens, query_latent, keyval_latent, query_gain, keyval_gain, query_cotangent, keyval_cotangent,
        master_query_up, master_keyval_up, master_query_down, master_keyval_down,
        mean_query_up, mean_keyval_up, mean_query_down, mean_keyval_down,
        square_query_up, square_keyval_up, square_query_down, square_keyval_down,
    ) = args
    hbm = pl.BlockSpec(memory_space=pl.ANY)
    vmem = pl.BlockSpec(memory_space=pltpu.VMEM)

    def shape(rows, cols, kind=f32):
        return jax.ShapeDtypeStruct((rows, cols), kind)

    V = pltpu.VMEM
    outs = pl.pallas_call(
        kernel,
        name="backward_and_update",
        out_shape=(
            shape(DC, TOK, bf16),
            shape(QR, QC), shape(KR, KC), shape(QR, DC), shape(KR, DC),
            shape(QR, QC), shape(KR, KC), shape(QR, DC), shape(KR, DC),
            shape(1, 8), shape(1, 8), shape(1, QR), shape(1, KR),
        ),
        in_specs=[hbm] * 3 + [vmem] * 2 + [hbm] * 10 + [vmem] * 4,
        out_specs=(hbm,) * 9 + (vmem,) * 4,
        scratch_shapes=[
            V((DC, TOK), bf16), V((TOK, QL), bf16), V((TOK, KVL), bf16), V((TOK, QC), bf16), V((TOK, KC), bf16),
            V((QR, QC), f32), V((KR, KC), f32), V((DR, DC), f32),
            V((QR, QC), f32), V((KR, KC), f32), V((DR, DC), f32),
            V((4, 4, QR, QC), bf16), V((4, 4, KR, KC), bf16), V((4, 4, DR, DC), bf16),
            V((16, QR, QC), bf16), V((16, KR, KC), bf16), V((4, 4, DR, DC), bf16),
            V((8, QR, QC), bf16), V((8, KR, KC), bf16), V((8, DR, DC), bf16),
            V((2, 4, QR, QC), bf16), V((2, 4, KR, KC), bf16), V((2, 4, DR, DC), bf16),
            V((TOK, QL), bf16), V((TOK, KVL), bf16), V((GW, TOK), bf16),
            V((4, TOK, GW), bf16), V((4, 320, GW), bf16), V((4, 320, GW), bf16),
            V((4, 3, SLICE, GW), bf16), V((4, SLICE, GW), bf16), V((4, SLICE, GW), bf16), V((4, SLICE, GW), f32),
            V((4, SLICE, GW), f32), V((4, 8, GW), f32),
            V((TOK, 4 * GW), bf16), V((DC, TOK), bf16),
            V((8, 128), f32), V((8, 128), f32), V((8, 8, 128), f32), V((8, 128), f32),
            V((2, 8, 128), f32), V((2, 8, 128), f32), V((4, 8, 128), f32),
            pltpu.SemaphoreType.DMA((N_SEM,)), pltpu.SemaphoreType.DMA((N_SEM,)), pltpu.SemaphoreType.DMA((32,)),
        ],
        compiler_params=pltpu.CompilerParams(
            collective_id=0, has_side_effects=True, vmem_limit_bytes=62 * 2**20
        ),
        cost_estimate=pl.CostEstimate(flops=11 * 10**9, bytes_accessed=14 * 10**6, transcendentals=0),
    )(
        tokens.T, query_latent, keyval_latent, query_gain.reshape(1, QL), keyval_gain.reshape(1, KVL),
        query_cotangent, keyval_cotangent,
        master_query_up, master_keyval_up, master_query_down, master_keyval_down,
        mean_query_up, mean_keyval_up, mean_query_down, mean_keyval_down,
        square_query_up.reshape(1, 8), square_keyval_up.reshape(1, 8),
        square_query_down.reshape(1, QR), square_keyval_down.reshape(1, KR),
    )
    return (
        outs[0].T, *outs[1:9],
        outs[9].reshape(8), outs[10].reshape(8), outs[11].reshape(QR), outs[12].reshape(KR),
    )


def solution(mesh):
    both = P("dp", "head")
    return jax.shard_map(
        local,
        mesh=mesh,
        in_specs=(both, P("dp", None), P("dp", None), P(), P()) + (both,) * 10
        + (P("head"), P("head"), P("dp"), P("dp")),
        out_specs=(both,) * 9 + (P("head"), P("head"), P("dp"), P("dp")),
        check_vma=False,
    )
```

time: 1310 us -> 201 us (0.15); the launches traced: 1300 us -> 200 us
  waiting for transfers between devices: 1110 us -> 0 us
  Pallas kernels: 0 us -> 187 us
  blocking collectives: 103 us -> 0 us
  matrix products: 32.6 us -> 0 us
  other arithmetic: 26 us -> 0 us
  between operations: 14.3 us -> 0.72 us
    reduce_scatter x4 -> x0, waiting for transfers between devices: 783 us -> none  [the longest x1 217 us: local(): lax.psum_scatter(part_query_up.astype(jnp.bfloat16), 'dp', scatter_dimens...]
    all_gather x3 -> x0, waiting for transfers between devices: 203 us -> none  [the longest x1 100 us: local(): lax.all_gather(master_query_up.astype(jnp.bfloat16), 'dp', axis=0, tiled=...]
    pallas_call x0 -> x1, Pallas kernels: none -> 187 us  [local(): pl.pallas_call(kernel, name='backward_and_update', out_shape=(shape(DC, T...]
    psum x1 -> x0, waiting for transfers between devices: 128 us -> none  [local(): lax.psum(query_upstream.astype(jnp.bfloat16), 'head').astype(jnp.float32)]
    psum x2 -> x0, blocking collectives: 63.5 us -> none  [the longest x1 32.4 us: local(): row_query, row_keyval = lax.psum((row_query, row_keyval), 'head')]
    all_gather x1 -> x0, blocking collectives: 39.9 us -> none  [local(): lax.all_gather(master_keyval_down.astype(jnp.bfloat16), 'dp', axis=0, til...]
    dot_general x8 -> x0, matrix products: 32.6 us -> none  [the longest x4 16 us: rows_product(): lax.dot_general(left, right, (((0,), (0,)), ((), ())), preferred_element_...]
  transfers between devices with their start and end apart: 8 -> 0, of which waited for: 8 -> 0; matrix products, arithmetic and copies ran while one was open for 3% -> 0% of each run, Pallas kernels for 0% -> 0%
where the time goes in v1:
time: 201 us; the launch traced here: 200 us
  Pallas kernels  187 us (93%)
  local copies, waits for them, and re-layouts  12.2 us (6%)
    pallas_call x1, Pallas kernels, local(): pl.pallas_call(kernel, name='backward_and_update', out_shape=(shape(DC, T...  187 us
    unnamed x35, local copies, waits for them, and re-layouts  10.9 us

profile of v1, /device:TPU:1, one launch (start us, length us, event | category | flops | bytes accessed | tf_op | source)
XLA Modules:
  0.0 200.0 jit_solution(13115421927358861296)
XLA Ops:
  0.6 1.3 reshape.56.gq_ref
  1.9 187.0 %backward_and_update.1 = (bf16[448,640]{1,0:T(8,128)(2,1)}, f32[96,1536]{1,0:T(8,128)}, f32[32,2048]{1,0:T(8,128)}, f32[96,448]{1,0:T(8,128)}, f32[32,448]{1,0:T...) custom-call(bf16[448,640]{1,0:T(8,128)(2,1)} %bitcast.12, ...), custom_call_target="tpu_custom_call" | custom-call | flops 11000000512 | bytes 14000000 | tf_op jit(solution)/shard_map/backward_and_update/pallas_call | solution.py:588
  189.0 0.0 copy-start.2
  189.0 0.0 copy-start.4
  189.0 0.0 copy-start.6
  189.0 0.0 copy-start
  189.0 2.0 %copy.45 = bf16[640,448]{0,1:T(8,128)(2,1)} copy(bf16[640,448]{0,1:T(8,128)(2,1)} %bitcast.11) | data formatting | bytes 1146880
  191.0 0.0 copy-start.1
  191.0 0.0 copy-start.3
  191.0 0.0 copy-start.5
  191.0 0.0 copy-start.10
  191.0 0.0 copy-start.9
  191.1 0.0 copy-start.8
  191.1 0.0 copy-start.7
  191.1 2.0 copy.46
  193.0 0.0 copy-done.2
  193.0 0.7 copy.47
  193.7 0.0 copy-done.4
  193.7 0.7 copy.48
  194.4 0.0 copy-done.6
  194.4 0.6 copy.49
  195.1 0.0 copy-done
  195.1 0.8 copy.50
  195.9 0.0 copy-done.1
  195.9 0.7 copy.51
  196.6 0.0 copy-done.3
  196.6 0.7 copy.52
  197.3 0.0 copy-done.5
  197.3 0.6 copy.53
  197.9 0.0 copy-done.10
  197.9 0.5 copy.54
  198.4 0.0 copy-done.9
  198.4 0.5 copy.55
  198.9 0.0 copy-done.8
  198.9 0.5 copy.56
  199.4 0.0 copy-done.7
  199.4 0.5 copy.57
Async XLA Ops:
  189.0 4.1 %copy-start.2 = (f32[32,2048]{1,0:T(8,128)S(1)}, f32[32,2048]{1,0:T(8,128)}, u32[]{:S(2)}) copy-start(f32[32,2048]{1,0:T(8,128)} %get-tuple-element.54) | copy-start | bytes 786436
  189.0 4.8 %copy-start.4 = (f32[96,448]{1,0:T(8,128)S(1)}, f32[96,448]{1,0:T(8,128)}, u32[]{:S(2)}) copy-start(f32[96,448]{1,0:T(8,128)} %get-tuple-element.55) | copy-start | bytes 516100
  189.0 5.4 %copy-start.6 = (f32[32,448]{1,0:T(8,128)S(1)}, f32[32,448]{1,0:T(8,128)}, u32[]{:S(2)}) copy-start(f32[32,448]{1,0:T(8,128)} %get-tuple-element.56) | copy-start | bytes 172036
  189.0 6.0 %copy-start = (f32[96,1536]{1,0:T(8,128)S(1)}, f32[96,1536]{1,0:T(8,128)}, u32[]{:S(2)}) copy-start(f32[96,1536]{1,0:T(8,128)} %get-tuple-element.57) | copy-start | bytes 1769476
  191.0 4.8 %copy-start.1 = (f32[32,2048]{1,0:T(8,128)S(1)}, f32[32,2048]{1,0:T(8,128)}, u32[]{:S(2)}) copy-start(f32[32,2048]{1,0:T(8,128)} %get-tuple-element.58) | copy-start | bytes 786436
  191.0 5.6 %copy-start.3 = (f32[96,448]{1,0:T(8,128)S(1)}, f32[96,448]{1,0:T(8,128)}, u32[]{:S(2)}) copy-start(f32[96,448]{1,0:T(8,128)} %get-tuple-element.59) | copy-start | bytes 516100
  191.0 6.2 %copy-start.5 = (f32[32,448]{1,0:T(8,128)S(1)}, f32[32,448]{1,0:T(8,128)}, u32[]{:S(2)}) copy-start(f32[32,448]{1,0:T(8,128)} %get-tuple-element.60) | copy-start | bytes 172036
  191.0 6.9 %copy-start.10 = (f32[1,8]{1,0:T(1,128)S(1)}, f32[1,8]{1,0:T(1,128)}, u32[]{:S(2)}) copy-start(f32[1,8]{1,0:T(1,128)} %get-tuple-element.35) | copy-start | bytes 100
  191.0 7.4 %copy-start.9 = (f32[1,8]{1,0:T(1,128)S(1)}, f32[1,8]{1,0:T(1,128)}, u32[]{:S(2)}) copy-start(f32[1,8]{1,0:T(1,128)} %get-tuple-element.36) | copy-start | bytes 100
  191.1 7.9 %copy-start.8 = (f32[1,96]{1,0:T(1,128)S(1)}, f32[1,96]{1,0:T(1,128)}, u32[]{:S(2)}) copy-start(f32[1,96]{1,0:T(1,128)} %get-tuple-element.37) | copy-start | bytes 1156
  191.1 8.4 %copy-start.7 = (f32[1,32]{1,0:T(1,128)S(1)}, f32[1,32]{1,0:T(1,128)}, u32[]{:S(2)}) copy-start(f32[1,32]{1,0:T(1,128)} %get-tuple-element.38) | copy-start | bytes 388

commit v2 on v1

--- a/solution.py
+++ b/solution.py
@@ -291,27 +291,6 @@
 
         loop(2, chunk)
 
-    order = (4, 3, 5, 2, 6, 1, 7, 0)
-    l_lk.wait()
-    normalize(lk, gk_ref, normk, KVL)
-    l_ck.wait()
-    part_keyval(1 - yh)
-    for d in order[:3]:
-        scatter_pair("k", d)
-    l_lq.wait()
-    normalize(lq, gq_ref, normq, QL)
-    gather_first("k", 1)
-    l_cq.wait()
-    part_query(1 - yh)
-    gather_first("q", 1)
-    for i, d in enumerate(order):
-        scatter_pair("q", d)
-        if i >= 3:
-            scatter_pair("k", d)
-    gather_pair("d")
-    part_keyval(yh)
-    part_query(yh)
-
     first_token = pl.multiple_of(c * (TOK // 2) + x * SLICE, 16)
 
     def arrange(src, gain_ref, rows, natural, width, group, at):
@@ -327,7 +306,7 @@
         gain = jnp.broadcast_to(gain_ref[...], (8, width))
         gains[group, :, at] = select_dot(gain, chosen)
 
-    for g in range(4):
+    def arrange_group(g):
         arrange(lq, gq_ref, QR, 0, QL, g, pl.ds(0, GQ))
         arrange(lk, gk_ref, KR, 0, KVL, g, pl.ds(GQ, GK))
 
@@ -360,37 +339,79 @@
         recv(("l", g), pair_in.at[g])
         add_into([mine.at[g], pair_in.at[g]], full.at[g], 0, SLICE)
 
-    for step in (1, 2, 3):
-        for rel in range(2):
-            for w in ("k", "q"):
-                gather_next(w, rel, step)
-        upstream(step)
-        if step > 1:
-            after_x(step - 1)
-        if step > 2:
-            after_low(step - 2)
-        after_core(step)
-
+    l_lk.wait()
+    normalize(lk, gk_ref, normk, KVL)
+    l_ck.wait()
+    part_keyval(1 - yh)
+    for d in (4, 3, 5):
+        scatter_pair("k", d)
+    gather_first("k", 1)
+    l_lq.wait()
+    normalize(lq, gq_ref, normq, QL)
+    gather_first("q", 1)
+    gather_next("k", 0, 1)
+    gather_next("q", 0, 1)
+    l_cq.wait()
+    part_query(1 - yh)
+    scatter_pair("q", 4)
+    gather_next("k", 1, 1)
+    gather_next("q", 1, 1)
+    scatter_pair("q", 3)
+    upstream(1)
+    after_core(1)
+
+    gather_next("k", 0, 2)
+    part_keyval(yh)
+    gather_next("q", 0, 2)
+    scatter_pair("q", 5)
+    gather_next("k", 1, 2)
+    scatter_pair("k", 2)
+    gather_next("q", 1, 2)
+    after_x(1)
+    scatter_pair("q", 2)
+    upstream(2)
+    after_core(2)
+
+    gather_next("k", 0, 3)
+    part_query(yh)
+    gather_next("q", 0, 3)
+    scatter_pair("k", 6)
+    gather_next("k", 1, 3)
+    scatter_pair("q", 6)
+    arrange_group(0)
+    arrange_group(1)
+    gather_next("q", 1, 3)
+    after_x(2)
+    scatter_pair("q", 1)
+    upstream(3)
+    after_core(3)
+
+    gather_next("k", 0, 4)
+    gather_next("q", 0, 4)
+    scatter_pair("k", 1)
+    scatter_first("k")
+    gather_next("k", 1, 4)
+    scatter_first("q")
+    after_low(1)
+    gather_next("q", 1, 4)
+    gather_first("d", 0)
+    upstream(0)
     after_x(3)
-    after_low(2)
-    for w in ("k", "q"):
-        gather_next(w, 0, 4)
-    scatter_first("k")
-    for w in ("k", "q"):
-        gather_next(w, 1, 4)
-    scatter_first("q")
-    upstream(0)
-    gather_first("d", 0)
-    gather_first("d", 1)
-    after_low(3)
+    scatter_pair("k", 7)
     scatter_next("k", 0)
     after_core(0)
     scatter_next("q", 0)
-    for rel in range(2):
-        gather_next("d", rel, 1)
+    gather_next("d", 0, 1)
     after_x(0)
+    scatter_pair("q", 7)
+    scatter_pair("k", 0)
+    gather_pair("d")
+    scatter_pair("q", 0)
+    arrange_group(2)
+    arrange_group(3)
     scatter_next("k", 1)
-    after_low(0)
+    for g in (2, 3, 0):
+        after_low(g)
 
     own_rows = pl.ds(first_token, SLICE)
 
@@ -430,8 +451,7 @@
         view = slope.at[block_rows(back, c), sides[side]]
         recv(("a", 1, side, 0), view)
         send(("a", 2, side), view, view, x_next[side])
-    for rel in range(2):
-        gather_next("d", rel, 2)
+    gather_next("d", 0, 2)
     scatter_next("k", 2)
     for side, back in ((0, -1), (1, 1)):
         recv(("a", 1, side, 1), slope.at[block_rows(back, c), sides[1 - side]])
@@ -441,6 +461,7 @@
         recv(("a", 2, side), slope.at[block_rows(2, c), sides[side]])
     view = slope.at[block_rows(2, c), :]
     send(("ac", 3), view, view, other_core)
+    scatter_next("q", 2)
     for i, k in enumerate((0, -1, 1, 2)):
         recv(("ac", i), slope.at[block_rows(k, 1 - c), :])
 
@@ -450,11 +471,9 @@
         out = dot_t(turned[...], tok[...]).astype(bf16)
         pd[g, :, pl.ds(0, QR), :] = out[:GQ].reshape(4, QR, DC)
         pd[g, :, pl.ds(QR, KR), :] = out[GQ:].reshape(4, KR, DC)
-    for d in order:
+    for d in (4, 3, 5, 2):
         scatter_pair("d", d)
-    scatter_next("q", 2)
-    for rel in range(2):
-        gather_next("d", rel, 3)
+    gather_next("d", 0, 3)
 
     def finish(refs, grad, mean, rows, cols):
         def step(i, squares):
@@ -479,20 +498,24 @@
     squares_k = finish(scatter_last("k"), None, ek, KR, KC)
     heads_k = jnp.sum(select_dot(squares_k, heads_of(KC, KVH)), axis=0, keepdims=True) / (KVL * KVH)
     scatter_first("d")
+    gather_first("d", 1)
     l_eq.wait()
     squares_q = finish(scatter_last("q"), None, eq, QR, QC)
     heads_q = jnp.sum(select_dot(squares_q, heads_of(QC, QK)), axis=0, keepdims=True) / (QL * QK)
     row8 = lax.broadcasted_iota(jnp.int32, (8, 128), 0)
     small[...] = jnp.where(row8 == 0, heads_q, jnp.where(row8 == 1, heads_k, 0.0))
     send(("hy",), small, small_pair, other_half)
+    for d in (6, 1, 7, 0):
+        scatter_pair("d", d)
     scatter_next("d", 0)
+    gather_next("d", 1, 1)
     recv(("hy",), small_pair)
     small_z[0] = small[...] + small_pair[...]
     for k in range(1, NZ):
         send(("hz", k), small_z.at[0], small_z.at[k], z_dev(k))
-
-    for rel in range(2):
-        gather_next("d", rel, 4)
+    gather_next("d", 0, 4)
+    scatter_next("d", 1)
+    gather_next("d", 1, 2)
 
     def token_grad(i):
         at = pl.ds(pl.multiple_of(i * 128, 128), 128)
@@ -501,10 +524,6 @@
             out += dot(slope[at, pl.ds(g * GW, GQ)], wd[g, :, pl.ds(0, QR), :].reshape(GQ, DC))
             out += dot(slope[at, pl.ds(g * GW + GQ, GK)], wd[g, :, pl.ds(QR, KR), :].reshape(GK, DC))
         tg[:, at] = out.T.astype(bf16)
-
-    loop(TOK // 128, token_grad)
-    stores = [fetch(tg, tg_h)]
-    scatter_next("d", 1)
 
     for k in range(1, NZ):
         recv(("hz", k), small_z.at[k])
@@ -529,9 +548,10 @@
 
     update(select_dot(second, columns_of(QC, QK))[0:1], eq, mq, QR)
     update(select_dot(second, columns_of(KC, KVH))[1:2], ek, mk, KR)
-    stores += [fetch(eq, nq_h), fetch(ek, nk_h), fetch(mq, uq_h), fetch(mk, uk_h)]
+    stores = [fetch(eq, nq_h), fetch(ek, nk_h), fetch(mq, uq_h), fetch(mk, uk_h)]
 
     scatter_next("d", 2)
+    gather_next("d", 1, 3)
     eye = lax.broadcasted_iota(jnp.int32, (128, 128), 0) == lax.broadcasted_iota(jnp.int32, (128, 128), 1)
     small_row[...] = jnp.zeros((8, 128), f32)
     small_row[pl.ds(0, 1), pl.ds(0, QR)] = sdq_ref[...]
@@ -547,9 +567,12 @@
     small_core[0] = jnp.broadcast_to(row, (8, 128))
     send(("rc",), small_core.at[0], small_core.at[1], other_core)
     stores += [fetch(ed.at[pl.ds(0, QR)], ndq_h), fetch(ed.at[pl.ds(QR, KR)], ndk_h)]
+    gather_next("d", 1, 4)
     recv(("rc",), small_core.at[1])
     small_lo[0] = small_core[0] + small_core[1]
     send(("rl",), small_lo.at[0], small_lo.at[1], other_low)
+    loop(TOK // 128, token_grad)
+    stores += [fetch(tg, tg_h)]
     recv(("rl",), small_lo.at[1])
     small_x[0] = small_lo[0] + small_lo[1]
     for k in range(1, NX):
@@ -569,6 +592,19 @@
         copy.wait_send()
     for store in stores:
         store.wait()
+
+
+def publish(*refs):
+    n = (len(refs) - 2) // 3
+    into = [pltpu.make_async_copy(refs[i], refs[2 * n + i], refs[-2].at[i]) for i in range(n)]
+    out = [pltpu.make_async_copy(refs[2 * n + i], refs[n + i], refs[-1].at[i]) for i in range(n)]
+    for copy in into:
+        copy.start()
+    for i in range(n):
+        into[i].wait()
+        out[i].start()
+    for copy in out:
+        copy.wait()
 
 
 def local(*args):
@@ -625,6 +661,15 @@
         square_query_up.reshape(1, 8), square_keyval_up.reshape(1, 8),
         square_query_down.reshape(1, QR), square_keyval_down.reshape(1, KR),
     )
+    outs = pl.pallas_call(
+        publish,
+        name="publish",
+        out_shape=tuple(jax.ShapeDtypeStruct(o.shape, o.dtype) for o in outs),
+        in_specs=[hbm] * len(outs),
+        out_specs=(hbm,) * len(outs),
+        scratch_shapes=[V(o.shape, o.dtype) for o in outs]
+        + [pltpu.SemaphoreType.DMA((len(outs),)), pltpu.SemaphoreType.DMA((len(outs),))],
+    )(*outs)
     return (
         outs[0].T, *outs[1:9],
         outs[9].reshape(8), outs[10].reshape(8), outs[11].reshape(QR), outs[12].reshape(KR),

time: 201 us -> 156 us (0.78)
  Pallas kernels: 187 us -> 154 us
  local copies, waits for them, and re-layouts: 12.2 us -> 1.3 us
    pallas_call x1, Pallas kernels: 187 us -> 151 us  [local(): pl.pallas_call(kernel, name='backward_and_update', out_shape=(shape(DC, T...]
    unnamed x35 -> x0, local copies, waits for them, and re-layouts: 10.9 us -> none
    pallas_call x0 -> x1, Pallas kernels: none -> 2.84 us  [local(): pl.pallas_call(publish, name='publish', out_shape=tuple((jax.ShapeDtypeSt...]
where the time goes in v2:
time: 156 us
  Pallas kernels  154 us (99%)
    pallas_call x1, Pallas kernels, local(): pl.pallas_call(kernel, name='backward_and_update', out_shape=(shape(DC, T...  151 us

profile of v2, /device:TPU:1, one launch (start us, length us, event | category | flops | bytes accessed | tf_op | source)
XLA Modules:
  0.0 156.2 jit_solution(15860728614877357977)
XLA Ops:
  0.6 1.3 reshape.56.gq_ref
  1.9 151.4 %backward_and_update.1 = (bf16[448,640]{1,0:T(8,128)(2,1)}, f32[96,1536]{1,0:T(8,128)}, f32[32,2048]{1,0:T(8,128)}, f32[96,448]{1,0:T(8,128)}, f32[32,448]{1,0:T...) custom-call(bf16[448,640]{1,0:T(8,128)(2,1)} %bitcast.11, ...), custom_call_target="tpu_custom_call" | custom-call | flops 11000000512 | bytes 14000000 | tf_op jit(solution)/shard_map/backward_and_update/pallas_call | solution.py:624
  153.3 2.8 %publish.1 = (bf16[448,640]{1,0:T(8,128)(2,1)}, f32[96,1536]{1,0:T(8,128)}, f32[32,2048]{1,0:T(8,128)}, f32[96,448]{1,0:T(8,128)}, f32[32,448]{1,0:T(8,128)}, /*...) custom-call(bf16[448,640]{1,0:T(8,128)(2,1)} %get-tuple-element.39.r, ...), custom_call_target="tpu_custom_call" | custom-call | tf_op jit(solution)/shard_map/publish/pallas_call | solution.py:664

commit v3 on v2

--- a/solution.py
+++ b/solution.py
@@ -16,9 +16,11 @@
 NZ = 8
 NX = 4
 DC = 448
-QR, KR, DR = 96, 32, 128
+QR, KR, DR = 96, 32, 448
 GQ, GK, GW = 4 * QR, 4 * KR, 4 * (QR + KR)
 QC, KC = 1536, 2048
+DB = QR + KR
+FAR = 128
 SLICE = 80
 
 norm_eps = 1e-06
@@ -98,8 +100,8 @@
     tok, lq, lk, cq, ck, mq, mk, md, eq, ek, ed,
     wq, wk, wd, pq, pk, pd, yq, yk, yd, zq, zk, zd,
     normq, normk, turned, up, core_in, half, x_in, mine, pair_in, full,
-    latent, gains, slope, tg, small, small_pair, small_z, small_row, small_core, small_lo, small_x,
-    send_sems, recv_sems, local_sems,
+    latent, gains, by_block, raw, slope, tg, small, small_pair, small_z, small_row, small_core, small_x,
+    gq_row, gk_row, send_sems, recv_sems, local_sems,
 ):
     dp = lax.axis_index("dp")
     hd = lax.axis_index("head")
@@ -111,6 +113,10 @@
 
     def x_dev(k):
         return (dp, ((x + k + NX) % NX) * 4 + yl * 2 + c)
+
+    def head_dev(k):
+        low = 1 - yl if k >= NX else yl
+        return (dp, ((x + k) % NX) * 4 + low * 2 + c)
 
     other_half = ((1 - yh) * NZ + z, hd)
     other_low = (dp, x * 4 + (1 - yl) * 2 + c)
@@ -144,6 +150,8 @@
         copy.start()
         return copy
 
+    gq_row[...] = gq_ref[...].reshape(1, QL)
+    gk_row[...] = gk_ref[...].reshape(1, KVL)
     l_mk, l_mq = fetch(mk_h, mk), fetch(mq_h, mq)
     l_lk, l_ck = fetch(lk_h, lk), fetch(ck_h, ck)
     l_lq, l_cq = fetch(lq_h, lq), fetch(cq_h, cq)
@@ -153,8 +161,8 @@
     l_ed = (fetch(edq_h, ed.at[pl.ds(0, QR)]), fetch(edk_h, ed.at[pl.ds(QR, KR)]))
 
     barrier = pltpu.get_barrier_semaphore()
-    peers = [z_dev(k) for k in range(1, NZ)] + [x_dev(k) for k in range(1, NX)]
-    peers += [other_half, other_low, other_core]
+    peers = [z_dev(k) for k in range(1, NZ)] + [head_dev(k) for k in range(1, 2 * NX)]
+    peers += [other_half, other_core]
     for dev in peers:
         pl.semaphore_signal(barrier, inc=1, device_id=dev, device_id_type=MESH)
 
@@ -170,27 +178,44 @@
     def gather_pair(w):
         ref, _ = gathered[w]
         send(("y", w), ref.at[place(0, 0)], ref.at[place(1, 0)], other_half)
+
+    def round_z(w, rel, ref):
+        return ref.at[:, pl.ds(0, QC - FAR)] if w == "q" and rel else ref
 
     def gather_first(w, rel):
         ref, _ = gathered[w]
         if rel:
             recv(("y", w), ref.at[place(1, 0)])
         for side, sign in ((0, -1), (1, 1)):
-            send(("g", w, rel, 1, side), ref.at[place(rel, 0)], ref.at[place(rel, sign)], z_next[side])
+            here, there = ref.at[place(rel, 0)], ref.at[place(rel, sign)]
+            send(("g", w, rel, 1, side), round_z(w, rel, here), round_z(w, rel, there), z_next[side])
+
+    def cross(d):
+        far = pl.ds(QC - FAR, FAR)
+        send(("b", d), wq.at[place(0, d)].at[:, far], wq.at[place(1, d)].at[:, far], other_half)
+
+    def crossed(d):
+        recv(("b", d), wq.at[place(1, d)].at[:, pl.ds(QC - FAR, FAR)])
 
     def gather_next(w, rel, step):
         ref, rows = gathered[w]
         h = rows // 2
         for side, sign in ((0, -1), (1, 1)):
-            here = ref.at[place(rel, sign * step)]
+            here = round_z(w, rel, ref.at[place(rel, sign * step)])
             if step == 4:
                 recv(("g", w, rel, 4, side), here.at[pl.ds(side * h, h)])
                 continue
             recv(("g", w, rel, step, side), here)
-            there = ref.at[place(rel, sign * (step + 1))]
+            there = round_z(w, rel, ref.at[place(rel, sign * (step + 1))])
             if step == 3:
                 here, there = here.at[pl.ds(side * h, h)], there.at[pl.ds(side * h, h)]
             send(("g", w, rel, step + 1, side), here, there, z_next[side])
+        if w == "q" and rel == 0 and step < 4:
+            cross(step)
+            cross(NZ - step)
+
+    def far_half(d, side):
+        return wq.at[place(1, d)].at[pl.ds(side * (QR // 2), QR // 2), pl.ds(QC - FAR, FAR)]
 
     def own_block(ref, half_of, d):
         return ref.at[half_of * NZ + (z + d) % NZ]
@@ -249,16 +274,16 @@
     gather_first("q", 0)
     for load in l_md:
         load.wait()
-    round_rows(md, wd.at[place(0, 0)], DR)
+    wd[place(0, 0)] = md[...].T.astype(bf16)
 
     def normalize(src, gain_ref, dst, width):
         def body(i):
-            at = pl.ds(pl.multiple_of(i * 16, 16), 16)
+            at = pl.ds(pl.multiple_of(i * 32, 32), 32)
             values = src[at, :].astype(f32)
             inverse = lax.rsqrt(jnp.sum(values * values, axis=1, keepdims=True) / width + norm_eps)
             dst[at, :] = (values * inverse * gain_ref[...]).astype(bf16)
 
-        loop(TOK // 16, body)
+        loop(TOK // 32, body)
 
     def turn(src, start, width):
         def body(i):
@@ -306,11 +331,27 @@
         gain = jnp.broadcast_to(gain_ref[...], (8, width))
         gains[group, :, at] = select_dot(gain, chosen)
 
+    def arrange_blocks():
+        col = lax.broadcasted_iota(jnp.int32, (1, GW), 1)
+        j = sum((col >= DB * k).astype(jnp.int32) for k in (1, 2, 3))
+        inside = col - j * DB
+        source = jnp.where(inside < QR, j * QR + inside, GQ + j * KR + inside - QR)
+        by_block[...] = (lax.broadcasted_iota(jnp.int32, (GW, GW), 0) == source).astype(f32).astype(bf16)
+
     def arrange_group(g):
-        arrange(lq, gq_ref, QR, 0, QL, g, pl.ds(0, GQ))
-        arrange(lk, gk_ref, KR, 0, KVL, g, pl.ds(GQ, GK))
+        arrange(lq, gq_row, QR, 0, QL, g, pl.ds(0, GQ))
+        arrange(lk, gk_row, KR, 0, KVL, g, pl.ds(GQ, GK))
 
     def upstream(g):
+        if g:
+            crossed(g)
+            crossed(NZ - g)
+        for side, d in ((0, -3), (1, 3)):
+            if g == 3:
+                send(("bf", side), far_half(d, side), far_half(4, side), z_next[side])
+            if g == 0:
+                recv(("bf", side), far_half(4, side))
+
         def body(i):
             at = pl.ds(pl.multiple_of(i * 160, 160), 160)
             up[g, at, pl.ds(0, GQ)] = dot_t(cq[at, :], wq[g].reshape(GQ, QC)).astype(bf16)
@@ -340,14 +381,14 @@
         add_into([mine.at[g], pair_in.at[g]], full.at[g], 0, SLICE)
 
     l_lk.wait()
-    normalize(lk, gk_ref, normk, KVL)
+    normalize(lk, gk_row, normk, KVL)
     l_ck.wait()
     part_keyval(1 - yh)
     for d in (4, 3, 5):
         scatter_pair("k", d)
     gather_first("k", 1)
     l_lq.wait()
-    normalize(lq, gq_ref, normq, QL)
+    normalize(lq, gq_row, normq, QL)
     gather_first("q", 1)
     gather_next("k", 0, 1)
     gather_next("q", 0, 1)
@@ -358,9 +399,9 @@
     gather_next("q", 1, 1)
     scatter_pair("q", 3)
     upstream(1)
+
+    gather_next("k", 0, 2)
     after_core(1)
-
-    gather_next("k", 0, 2)
     part_keyval(yh)
     gather_next("q", 0, 2)
     scatter_pair("q", 5)
@@ -370,25 +411,25 @@
     after_x(1)
     scatter_pair("q", 2)
     upstream(2)
+
+    gather_next("k", 0, 3)
     after_core(2)
-
-    gather_next("k", 0, 3)
     part_query(yh)
     gather_next("q", 0, 3)
     scatter_pair("k", 6)
     gather_next("k", 1, 3)
     scatter_pair("q", 6)
+    arrange_blocks()
     arrange_group(0)
     arrange_group(1)
     gather_next("q", 1, 3)
     after_x(2)
     scatter_pair("q", 1)
     upstream(3)
+
+    gather_next("k", 0, 4)
     after_core(3)
-
-    gather_next("k", 0, 4)
     gather_next("q", 0, 4)
-    scatter_pair("k", 1)
     scatter_first("k")
     gather_next("k", 1, 4)
     scatter_first("q")
@@ -397,12 +438,13 @@
     gather_first("d", 0)
     upstream(0)
     after_x(3)
-    scatter_pair("k", 7)
     scatter_next("k", 0)
     after_core(0)
     scatter_next("q", 0)
     gather_next("d", 0, 1)
     after_x(0)
+    scatter_pair("k", 1)
+    scatter_pair("k", 7)
     scatter_pair("q", 7)
     scatter_pair("k", 0)
     gather_pair("d")
@@ -417,7 +459,6 @@
 
     def norm_back(i):
         at = pl.ds(pl.multiple_of(i * 16, 16), 16)
-        to = pl.ds(pl.multiple_of(first_token + i * 16, 16), 16)
         for first, width, units in ((0, GQ, QL), (GQ, GK, KVL)):
             cols = pl.ds(first, width)
             squares = 0.0
@@ -430,9 +471,12 @@
             scale = inverse * inverse * inverse * (inner / units)
             for g in range(4):
                 weighted = gains[g, pl.ds(0, 1), cols] * full[g, at, cols]
-                slope[to, pl.ds(g * GW + first, width)] = (inverse * weighted - latent[g, at, cols] * scale).astype(bf16)
+                raw[at, pl.ds(g * GW + first, width)] = (inverse * weighted - latent[g, at, cols] * scale).astype(bf16)
 
     loop(SLICE // 16, norm_back)
+    for g in range(4):
+        cols = pl.ds(g * GW, GW)
+        slope[own_rows, cols] = dot(raw[:, cols], by_block[...]).astype(bf16)
 
     sides = (pl.ds(0, 2 * GW), pl.ds(2 * GW, 2 * GW))
 
@@ -466,13 +510,12 @@
         recv(("ac", i), slope.at[block_rows(k, 1 - c), :])
 
     l_tok.wait()
-    for g in range(4):
-        turn(slope, g * GW, GW)
-        out = dot_t(turned[...], tok[...]).astype(bf16)
-        pd[g, :, pl.ds(0, QR), :] = out[:GQ].reshape(4, QR, DC)
-        pd[g, :, pl.ds(QR, KR), :] = out[GQ:].reshape(4, KR, DC)
-    for d in (4, 3, 5, 2):
-        scatter_pair("d", d)
+    for g, partners in ((0, (4,)), (3, (3, 5)), (2, (2,)), (1, ())):
+        out = dot(tok[...], slope[:, pl.ds(g * GW, GW)]).astype(bf16)
+        for j in range(4):
+            pd[g, j] = out[:, j * DB : (j + 1) * DB]
+        for d in partners:
+            scatter_pair("d", d)
     gather_next("d", 0, 3)
 
     def finish(refs, grad, mean, rows, cols):
@@ -517,13 +560,12 @@
     scatter_next("d", 1)
     gather_next("d", 1, 2)
 
-    def token_grad(i):
-        at = pl.ds(pl.multiple_of(i * 128, 128), 128)
-        out = jnp.zeros((128, DC), f32)
+    def token_grad():
+        out = jnp.zeros((DC, TOK), f32)
         for g in range(4):
-            out += dot(slope[at, pl.ds(g * GW, GQ)], wd[g, :, pl.ds(0, QR), :].reshape(GQ, DC))
-            out += dot(slope[at, pl.ds(g * GW + GQ, GK)], wd[g, :, pl.ds(QR, KR), :].reshape(GK, DC))
-        tg[:, at] = out.T.astype(bf16)
+            rows = jnp.concatenate([wd[g, j] for j in range(4)], axis=1)
+            out += dot_t(rows, slope[:, pl.ds(g * GW, GW)])
+        tg[...] = out.astype(bf16)
 
     for k in range(1, NZ):
         recv(("hz", k), small_z.at[k])
@@ -559,7 +601,7 @@
     old = small_row[pl.ds(0, 1), :]
     for load in l_ed:
         load.wait()
-    grad = total(scatter_last("d"), slice(None)) / TOKENS
+    grad = total(scatter_last("d"), slice(None)).T / TOKENS
     mean_next = beta_first * ed[...] + (1.0 - beta_first) * grad
     ed[...] = mean_next
     column = jnp.sum(grad * grad, axis=1, keepdims=True) / D
@@ -569,20 +611,19 @@
     stores += [fetch(ed.at[pl.ds(0, QR)], ndq_h), fetch(ed.at[pl.ds(QR, KR)], ndk_h)]
     gather_next("d", 1, 4)
     recv(("rc",), small_core.at[1])
-    small_lo[0] = small_core[0] + small_core[1]
-    send(("rl",), small_lo.at[0], small_lo.at[1], other_low)
-    loop(TOK // 128, token_grad)
+    small_x[0] = small_core[0] + small_core[1]
+    for k in range(1, 2 * NX):
+        send(("rx", k), small_x.at[0], small_x.at[k], head_dev(k))
+    token_grad()
     stores += [fetch(tg, tg_h)]
-    recv(("rl",), small_lo.at[1])
-    small_x[0] = small_lo[0] + small_lo[1]
-    for k in range(1, NX):
-        send(("rx", k), small_x.at[0], small_x.at[k], x_dev(k))
-    for k in range(1, NX):
+    for k in range(1, 2 * NX):
         recv(("rx", k), small_x.at[k])
-    rows_total = (small_x[0] + small_x[1]) + (small_x[2] + small_x[3])
+    rows_total = small_x[0]
+    for k in range(1, 2 * NX):
+        rows_total = rows_total + small_x[k]
     second_row = beta_second * old + (1.0 - beta_second) * rows_total[0:1]
     osdq_ref[...] = second_row[:, 0:QR]
-    osdk_ref[...] = second_row[:, QR:DR]
+    osdk_ref[...] = second_row[:, QR:DB]
     second_col = jnp.sum(jnp.where(eye, second_row, 0.0), axis=1, keepdims=True)
     factor = 1.0 / (jnp.sqrt(second_col / second_scale) + adam_eps)
     md[...] = mean_next / first_scale * factor
@@ -634,19 +675,20 @@
         out_specs=(hbm,) * 9 + (vmem,) * 4,
         scratch_shapes=[
             V((DC, TOK), bf16), V((TOK, QL), bf16), V((TOK, KVL), bf16), V((TOK, QC), bf16), V((TOK, KC), bf16),
-            V((QR, QC), f32), V((KR, KC), f32), V((DR, DC), f32),
-            V((QR, QC), f32), V((KR, KC), f32), V((DR, DC), f32),
-            V((4, 4, QR, QC), bf16), V((4, 4, KR, KC), bf16), V((4, 4, DR, DC), bf16),
-            V((16, QR, QC), bf16), V((16, KR, KC), bf16), V((4, 4, DR, DC), bf16),
-            V((8, QR, QC), bf16), V((8, KR, KC), bf16), V((8, DR, DC), bf16),
-            V((2, 4, QR, QC), bf16), V((2, 4, KR, KC), bf16), V((2, 4, DR, DC), bf16),
+            V((QR, QC), f32), V((KR, KC), f32), V((DB, DC), f32),
+            V((QR, QC), f32), V((KR, KC), f32), V((DB, DC), f32),
+            V((4, 4, QR, QC), bf16), V((4, 4, KR, KC), bf16), V((4, 4, DC, DB), bf16),
+            V((16, QR, QC), bf16), V((16, KR, KC), bf16), V((4, 4, DC, DB), bf16),
+            V((8, QR, QC), bf16), V((8, KR, KC), bf16), V((8, DC, DB), bf16),
+            V((2, 4, QR, QC), bf16), V((2, 4, KR, KC), bf16), V((2, 4, DC, DB), bf16),
             V((TOK, QL), bf16), V((TOK, KVL), bf16), V((GW, TOK), bf16),
             V((4, TOK, GW), bf16), V((4, 320, GW), bf16), V((4, 320, GW), bf16),
             V((4, 3, SLICE, GW), bf16), V((4, SLICE, GW), bf16), V((4, SLICE, GW), bf16), V((4, SLICE, GW), f32),
-            V((4, SLICE, GW), f32), V((4, 8, GW), f32),
+            V((4, SLICE, GW), f32), V((4, 8, GW), f32), V((GW, GW), bf16), V((SLICE, 4 * GW), bf16),
             V((TOK, 4 * GW), bf16), V((DC, TOK), bf16),
             V((8, 128), f32), V((8, 128), f32), V((8, 8, 128), f32), V((8, 128), f32),
-            V((2, 8, 128), f32), V((2, 8, 128), f32), V((4, 8, 128), f32),
+            V((2, 8, 128), f32), V((8, 8, 128), f32),
+            V((1, QL), f32), V((1, KVL), f32),
             pltpu.SemaphoreType.DMA((N_SEM,)), pltpu.SemaphoreType.DMA((N_SEM,)), pltpu.SemaphoreType.DMA((32,)),
         ],
         compiler_params=pltpu.CompilerParams(
@@ -654,7 +696,7 @@
         ),
         cost_estimate=pl.CostEstimate(flops=11 * 10**9, bytes_accessed=14 * 10**6, transcendentals=0),
     )(
-        tokens.T, query_latent, keyval_latent, query_gain.reshape(1, QL), keyval_gain.reshape(1, KVL),
+        tokens.T, query_latent, keyval_latent, query_gain, keyval_gain,
         query_cotangent, keyval_cotangent,
         master_query_up, master_keyval_up, master_query_down, master_keyval_down,
         mean_query_up, mean_keyval_up, mean_query_down, mean_keyval_down,

time: 156 us -> 151 us (0.968)
  Pallas kernels: 154 us -> 150 us
    pallas_call x1, Pallas kernels: 151 us -> 147 us  [local(): pl.pallas_call(kernel, name='backward_and_update', out_shape=(shape(DC, T...]
where the time goes in v3:
time: 151 us
  Pallas kernels  150 us (99%)
    pallas_call x1, Pallas kernels, local(): pl.pallas_call(kernel, name='backward_and_update', out_shape=(shape(DC, T...  147 us

profile of v3, /device:TPU:1, one launch (start us, length us, event | category | flops | bytes accessed | tf_op | source)
XLA Modules:
  0.0 150.7 jit_solution(3403808879530141729)
XLA Ops:
  0.7 147.1 %backward_and_update.1 = (bf16[448,640]{1,0:T(8,128)(2,1)}, f32[96,1536]{1,0:T(8,128)}, f32[32,2048]{1,0:T(8,128)}, f32[96,448]{1,0:T(8,128)}, f32[32,448]{1,0:T...) custom-call(bf16[448,640]{1,0:T(8,128)(2,1)} %bitcast.10, ...), custom_call_target="tpu_custom_call" | custom-call | flops 11000000512 | bytes 14000000 | tf_op jit(solution)/shard_map/backward_and_update/pallas_call | solution.py:665
  147.7 2.8 %publish.1 = (bf16[448,640]{1,0:T(8,128)(2,1)}, f32[96,1536]{1,0:T(8,128)}, f32[32,2048]{1,0:T(8,128)}, f32[96,448]{1,0:T(8,128)}, f32[32,448]{1,0:T(8,128)}, /*...) custom-call(bf16[448,640]{1,0:T(8,128)(2,1)} %get-tuple-element.39.r, ...), custom_call_target="tpu_custom_call" | custom-call | tf_op jit(solution)/shard_map/publish/pallas_call | solution.py:706

commit v4 on v3

--- a/solution.py
+++ b/solution.py
@@ -20,7 +20,7 @@
 GQ, GK, GW = 4 * QR, 4 * KR, 4 * (QR + KR)
 QC, KC = 1536, 2048
 DB = QR + KR
-FAR = 128
+FAR = 256
 SLICE = 80
 
 norm_eps = 1e-06
@@ -353,11 +353,11 @@
                 recv(("bf", side), far_half(4, side))
 
         def body(i):
-            at = pl.ds(pl.multiple_of(i * 160, 160), 160)
+            at = pl.ds(pl.multiple_of(i * 320, 320), 320)
             up[g, at, pl.ds(0, GQ)] = dot_t(cq[at, :], wq[g].reshape(GQ, QC)).astype(bf16)
             up[g, at, pl.ds(GQ, GK)] = dot_t(ck[at, :], wk[g].reshape(GK, KC)).astype(bf16)
 
-        loop(TOK // 160, body)
+        loop(TOK // 320, body)
         there = pl.ds(pl.multiple_of((1 - c) * 320, 16), 320)
         send(("c", g), up.at[g, there], core_in.at[g], other_core)
 

time: 151 us -> 148 us (0.980)
  Pallas kernels: 150 us -> 147 us
    pallas_call x1, Pallas kernels: 147 us -> 144 us  [local(): pl.pallas_call(kernel, name='backward_and_update', out_shape=(shape(DC, T...]
where the time goes in v4:
time: 148 us
  Pallas kernels  147 us (99%)
    pallas_call x1, Pallas kernels, local(): pl.pallas_call(kernel, name='backward_and_update', out_shape=(shape(DC, T...  144 us

profile of v4, /device:TPU:1, one launch (start us, length us, event | category | flops | bytes accessed | tf_op | source)
XLA Modules:
  0.0 147.9 jit_solution(18326307178565859545)
XLA Ops:
  0.7 144.3 %backward_and_update.1 = (bf16[448,640]{1,0:T(8,128)(2,1)}, f32[96,1536]{1,0:T(8,128)}, f32[32,2048]{1,0:T(8,128)}, f32[96,448]{1,0:T(8,128)}, f32[32,448]{1,0:T...) custom-call(bf16[448,640]{1,0:T(8,128)(2,1)} %bitcast.10, ...), custom_call_target="tpu_custom_call" | custom-call | flops 11000000512 | bytes 14000000 | tf_op jit(solution)/shard_map/backward_and_update/pallas_call | solution.py:665
  144.9 2.8 %publish.1 = (bf16[448,640]{1,0:T(8,128)(2,1)}, f32[96,1536]{1,0:T(8,128)}, f32[32,2048]{1,0:T(8,128)}, f32[96,448]{1,0:T(8,128)}, f32[32,448]{1,0:T(8,128)}, /*...) custom-call(bf16[448,640]{1,0:T(8,128)(2,1)} %get-tuple-element.39.r, ...), custom_call_target="tpu_custom_call" | custom-call | tf_op jit(solution)/shard_map/publish/pallas_call | solution.py:706

commit v5 on v4

--- a/solution.py
+++ b/solution.py
@@ -353,11 +353,11 @@
                 recv(("bf", side), far_half(4, side))
 
         def body(i):
-            at = pl.ds(pl.multiple_of(i * 320, 320), 320)
+            at = pl.ds(pl.multiple_of(i * 640, 640), 640)
             up[g, at, pl.ds(0, GQ)] = dot_t(cq[at, :], wq[g].reshape(GQ, QC)).astype(bf16)
             up[g, at, pl.ds(GQ, GK)] = dot_t(ck[at, :], wk[g].reshape(GK, KC)).astype(bf16)
 
-        loop(TOK // 320, body)
+        loop(TOK // 640, body)
         there = pl.ds(pl.multiple_of((1 - c) * 320, 16), 320)
         send(("c", g), up.at[g, there], core_in.at[g], other_core)
 

time: 148 us -> 148 us (level)
  no operation moved by 1% of the time
where the time goes in v5:
time: 148 us
  Pallas kernels  147 us (99%)
    pallas_call x1, Pallas kernels, local(): pl.pallas_call(kernel, name='backward_and_update', out_shape=(shape(DC, T...  144 us

profile of v5, /device:TPU:1, one launch (start us, length us, event | category | flops | bytes accessed | tf_op | source)
XLA Modules:
  0.0 147.8 jit_solution(7649695228130565374)
XLA Ops:
  0.7 144.1 %backward_and_update.1 = (bf16[448,640]{1,0:T(8,128)(2,1)}, f32[96,1536]{1,0:T(8,128)}, f32[32,2048]{1,0:T(8,128)}, f32[96,448]{1,0:T(8,128)}, f32[32,448]{1,0:T...) custom-call(bf16[448,640]{1,0:T(8,128)(2,1)} %bitcast.10, ...), custom_call_target="tpu_custom_call" | custom-call | flops 11000000512 | bytes 14000000 | tf_op jit(solution)/shard_map/backward_and_update/pallas_call | solution.py:665
  144.8 2.8 %publish.1 = (bf16[448,640]{1,0:T(8,128)(2,1)}, f32[96,1536]{1,0:T(8,128)}, f32[32,2048]{1,0:T(8,128)}, f32[96,448]{1,0:T(8,128)}, f32[32,448]{1,0:T(8,128)}, /*...) custom-call(bf16[448,640]{1,0:T(8,128)(2,1)} %get-tuple-element.39.r, ...), custom_call_target="tpu_custom_call" | custom-call | tf_op jit(solution)/shard_map/publish/pallas_call | solution.py:706
